TPU v7x, 256 devices: a whole 4x4x8 slice. The times are simulated.
256 devices in a mesh: img: 8 (over z_hi, y), mx: 8 (over z_lo, core), my: 4 (over x).
Axes of the slice: x: 4, y: 4, z: 8 (z_hi: 2, z_lo: 4; z = z_hi * 4 + z_lo), core: 2. Of those that a mesh axis runs over, the one named last changes fastest.
Arguments:
- patches: bfloat16 [8192, 6144], P(('img', 'my'), 'mx')
- tile_counts: int32 [16], replicated, may hold values from 1 to 4, as said below
- image_owner: int32 [16], replicated, may hold values from 0 to 7, as said below
- block_target: int32 [8, 8], P('img'), may hold values from 0 to 7, each once within a row
- qkv_weight: bfloat16 [6144, 3, 4096], P('mx', None, 'my')
- out_weight: bfloat16 [4096, 6144], P('my', 'mx'), may hold values from -0.09375 to 0.09375
Outputs:
- routed: bfloat16 [8192, 6144], P(('img', 'my'), 'mx')
Inputs may be any that keep to these rules, and one draw needn't show every extreme that they name: `tile_counts`: each image has 1 to 4 blocks; the two images of an arrival group fit its 8 blocks. `image_owner`: the owner of image k is k // 2 or the group whose index differs from it in the lowest bit; every group owns exactly two images, their blocks sum to at most 8, and in every draw some group owns exactly 8 blocks.
All inputs are finite; a program needn't handle non-finite values.
Results may differ from a plain program's by a relative error of at most 0.015.
Values may be sent and summed in bfloat16 or wider, within the bound.
No kernel may reach another device: no remote copies, remote signals or barrier semaphores. Data moves between devices by JAX's collectives and lax.ppermute only.
A program may use at most 128 MiB of HBM per device.

v0:
```python
import jax
import jax.numpy as jnp
from jax import lax
from jax.sharding import PartitionSpec as P

D = 6144
HD = 128
BLK = 128
BLK_GRP = 8
R = 1024


def partner(block, axis, distance):
    count = lax.axis_size(axis)
    route = []
    for low in range(count):
        high = low | 1 << distance
        if high != low and high < count:
            route += [(low, high), (high, low)]
    return lax.ppermute(block, axis, route)


def layout_blocks(tile_counts, image_owner, img_index, blocks):
    images = tile_counts.shape[0]
    positions = jnp.arange(images, dtype=jnp.int32)
    previous = jnp.concatenate([jnp.zeros((1,), jnp.int32), tile_counts[:-1]])
    first_block = jnp.where(positions % 2 == 1, previous, 0)
    source = positions // 2
    member = (image_owner == img_index).astype(jnp.int32)
    counted = member * tile_counts
    offset = jnp.cumsum(counted, dtype=jnp.int32) - counted
    slot_ids = jnp.arange(blocks, dtype=jnp.int32)[:, None]
    inside = (
        (member[None, :] == 1)
        & (slot_ids >= offset[None, :])
        & (slot_ids < offset[None, :] + tile_counts[None, :])
    )
    hit_table = inside.astype(jnp.int32)
    live_count = jnp.sum(hit_table, axis=1, dtype=jnp.int32)
    image_id = jnp.sum(hit_table * positions[None, :], axis=1, dtype=jnp.int32) + live_count - 1
    src_block = jnp.sum(
        hit_table * (first_block[None, :] + slot_ids - offset[None, :]), axis=1, dtype=jnp.int32
    )
    src_group = jnp.sum(hit_table * source[None, :], axis=1, dtype=jnp.int32)
    return (image_id, src_block, src_group)


def attend(queries, key_rows, value_rows, row_ids, block_rows):
    score_scale = queries.shape[1] ** (-0.5)
    valid_key = row_ids >= 0
    outputs = []
    for first_row in range(0, queries.shape[0], block_rows):
        query_block = queries[first_row : first_row + block_rows]
        block_ids = row_ids[first_row : first_row + block_rows]
        scores = (
            lax.dot_general(
                query_block, key_rows, (((1,), (1,)), ((), ())), preferred_element_type=jnp.float32
            )
            * score_scale
        )
        allowed = (block_ids[:, None] == row_ids[None, :]) & valid_key[None, :]
        scores = jnp.where(allowed, scores, jnp.float32(-1e30))
        row_top = jnp.max(scores, axis=1, keepdims=True)
        powers = jnp.exp(scores - row_top)
        weights = (powers / jnp.sum(powers, axis=1, keepdims=True)).astype(jnp.bfloat16)
        mixture = jnp.dot(weights, value_rows, preferred_element_type=jnp.float32)
        mixture = jnp.where((block_ids >= 0)[:, None], mixture, jnp.float32(0.0))
        outputs.append(mixture.astype(jnp.bfloat16))
    return jnp.concatenate(outputs, axis=0)


def shards(patches, tile_counts, image_owner, block_target, qkv_weight, out_weight):
    values = patches.astype(jnp.float32)
    row_sum, row_square = lax.psum(
        (jnp.sum(values, axis=1), jnp.sum(values * values, axis=1)), "mx"
    )
    mean_row = row_sum / D
    var_row = row_square / D - mean_row * mean_row
    normed = ((values - mean_row[:, None]) * lax.rsqrt(var_row[:, None] + 1e-06)).astype(
        jnp.bfloat16
    )
    img_index = lax.axis_index("img")
    own_rows = lax.all_gather(normed, "my", axis=0, tiled=True)
    partner_rows = partner(own_rows, "img", 0)
    image_id, src_block, src_group = layout_blocks(tile_counts, image_owner, img_index, BLK_GRP)
    local_block = jnp.where(src_group == img_index, src_block, BLK_GRP + src_block)
    columns = own_rows.shape[1]
    stacked = jnp.concatenate([own_rows, partner_rows], axis=0).reshape(2 * BLK_GRP, BLK, columns)
    packed = jnp.take(stacked, local_block, axis=0).reshape(R, columns)
    row_ids = jnp.repeat(image_id, BLK)
    partial_value = jnp.einsum(
        "rd,dcf->rcf", packed, qkv_weight, preferred_element_type=jnp.float32
    )
    qkv_rows = lax.psum_scatter(partial_value, "mx", scatter_dimension=2, tiled=True).astype(
        jnp.bfloat16
    )
    block_rows = min(512, R)
    attended = attend(
        qkv_rows[:, 0, 0:HD], qkv_rows[:, 1, 0:HD], qkv_rows[:, 2, 0:HD], row_ids, block_rows
    )
    heads_rows = lax.all_gather(attended, "mx", axis=1, tiled=True)
    targets = block_target[0]
    slot_ids = jnp.arange(BLK_GRP, dtype=jnp.int32)
    inverse = jnp.sum(
        jnp.where(targets[None, :] == slot_ids[:, None], slot_ids[None, :], 0),
        axis=1,
        dtype=jnp.int32,
    )
    feature_count = heads_rows.shape[1]
    routed_rows = jnp.take(
        heads_rows.reshape(BLK_GRP, BLK, feature_count), inverse, axis=0
    ).reshape(R, feature_count)
    return lax.psum_scatter(
        jnp.dot(routed_rows, out_weight, preferred_element_type=jnp.float32).astype(jnp.bfloat16),
        "my",
        scatter_dimension=0,
        tiled=True,
    )


def solution(mesh):
    in_specs = (
        P(("img", "my"), "mx"),
        P(),
        P(),
        P("img", None),
        P("mx", None, "my"),
        P("my", "mx"),
    )
    out_specs = P(("img", "my"), "mx")
    return jax.shard_map(shards, mesh=mesh, in_specs=in_specs, out_specs=out_specs, check_vma=False)
```

profile of v0, /device:TPU:1, one launch (start us, length us, event | category | flops | bytes accessed | tf_op | source)
XLA Modules:
  0.0 329.2 jit_solution(2877222204307457723)
XLA Ops:
  6.5 1.3 convert_reduce_fusion
  7.9 16.2 %all-reduce = (f32[256]{0:T(256)S(1)}, f32[256]{0:T(256)S(1)}) all-reduce(f32[256]{0:T(256)S(1)} %get-tuple-element.6, f32[256]{0:T(256)S(1)} %get-tuple-element.5), channel_id=1, replica_groups=mesh['img'=8,'mx'=8,'my'=4] {'mx'}, use_global_device_ids=true, to_apply=%region_9.10 | all-reduce | flops 512 | bytes 4096 | tf_op jit(solution)/shard_map/psum | solution.py:74
  24.1 2.0 fusion.7
  26.1 31.7 %all-gather.3.cloned.1.call-done = bf16[1024,768]{1,0:T(8,128)(2,1)} async-done(((bf16[256,768]{1,0:T(8,128)(2,1)}), bf16[1024,768]{1,0:T(8,128)(2,1)}) %all-gather.3.cloned.1.call-update) | async-done | bytes 1572880 | tf_op jit(solution)/shard_map/all_gather | solution.py:83
  57.8 1.2 collective-permute-start
  59.0 0.7 fusion.15
  60.0 0.7 compare_select_fusion.4
  60.7 0.7 fusion.11
  61.3 0.7 fusion.16
  62.3 31.0 %collective-permute-done = bf16[1024,768]{1,0:T(8,128)(2,1)S(1)} collective-permute-done((bf16[1024,768]{1,0:T(8,128)(2,1)}, bf16[1024,768]{1,0:T(8,128)(2,1)S(1)}, u32[]{:S(2)}, u32[]{:S(2)}) %collective-permute-start) | collective-permute-done | bytes 1572896 | tf_op jit(solution)/shard_map/ppermute | solution.py:20
  93.3 3.3 pad_maximum_fusion
  96.6 2.5 gather_fusion
  99.4 10.3 %fusion.2 = f32[1024,3,1024]{2,0,1:T(8,128)} fusion(bf16[768,3,1024]{2,0,1:T(8,128)(2,1)} %param.10, bf16[1024,768]{1,0:T(8,128)(2,1)S(1)} %bitcast_select_fusion.1), kind=kOutput, calls=%fused_computation.13 | convolution fusion | flops 4831838208 | bytes 18874368 | tf_op jit(solution)/shard_map/rd,dcf->rcf/dot_general | solution.py:91
  110.3 132.2 %reduce-scatter.3.cloned.1.call-done = f32[1024,3,128]{2,0,1:T(8,128)} async-done(((f32[1024,3,1024]{2,0,1:T(8,128)}), f32[1024,3,128]{2,0,1:T(8,128)}) %reduce-scatter.3.cloned.1.call-update) | async-done | bytes 1572880 | tf_op jit(solution)/shard_map/reduce_scatter | solution.py:94
  242.5 1.5 convert_element_type.34
  244.0 0.7 fusion.20
  244.7 0.7 fusion.19
  246.0 0.6 fusion.4
  247.6 0.7 pad_maximum_fusion.1
  248.6 40.3 %all-gather.5.cloned.1.call-done = bf16[1024,1024]{1,0:T(8,128)(2,1)} async-done(((bf16[1024,128]{1,0:T(8,128)(2,1)}), bf16[1024,1024]{1,0:T(8,128)(2,1)}) %all-gather.5.cloned.1.call-update) | async-done | bytes 2097168 | tf_op jit(solution)/shard_map/all_gather | solution.py:101
  289.0 3.6 %gather_fusion.1 = bf16[8,128,1024]{2,1,0:T(8,128)(2,1)} fusion(bf16[8,128,1024]{2,1,0:T(8,128)(2,1)} %bitcast.66, s32[1024]{0:T(1024)S(1)} %pad_clamp_fusion), kind=kCustom, calls=%fused_computation.1 | custom fusion | bytes 4194336 | tf_op jit(solution)/shard_map/jit(_take)/gather | solution.py:110
  292.5 1.9 bitcast_select_fusion
  294.4 3.0 convolution_convert_fusion
  297.4 25.3 %reduce-scatter.5.cloned.1.call-done = bf16[256,768]{1,0:T(8,128)(2,1)} async-done(((bf16[1024,768]{1,0:T(8,128)(2,1)}), bf16[256,768]{1,0:T(8,128)(2,1)}) %reduce-scatter.5.cloned.1.call-update) | async-done | bytes 393232 | tf_op jit(solution)/shard_map/reduce_scatter | solution.py:113
  (38 shorter events, 3.3 us)
Async XLA Ops:
  6.5 287.8 %copy-start = (bf16[1024,768]{1,0:T(8,128)(2,1)S(1)}, bf16[1024,768]{1,0:T(8,128)(2,1)}, u32[]{:S(2)}) copy-start(bf16[1024,768]{1,0:T(8,128)(2,1)} %param.11) | copy-start | bytes 4718596
  6.5 51.3 %all-gather.3.cloned.1.call-start = ((), (), s32[]{:S(2)}) async-start(), calls=%async_computation.2 | async-start | bytes 1966080 | tf_op jit(solution)/shard_map/all_gather | solution.py:83
  26.1 216.4 %reduce-scatter.3.cloned.1.call-start = ((), (), s32[]{:S(2)}) async-start(), calls=%async_computation.3 | async-start | bytes 14155776 | tf_op jit(solution)/shard_map/reduce_scatter | solution.py:94
  57.8 35.5 %collective-permute-start = (bf16[1024,768]{1,0:T(8,128)(2,1)}, bf16[1024,768]{1,0:T(8,128)(2,1)S(1)}, u32[]{:S(2)}, u32[]{:S(2)}) collective-permute-start(bf16[1024,768]{1,0:T(8,128)(2,1)} %all-gather.3.cloned.1.call-done), channel_id=1, source_target_pairs={{0,32},{32,0},{64,96},{96,64},{128,160},{160,128},{192,224},{224,1... | collective-permute-start | bytes 4718600 | tf_op jit(solution)/shard_map/ppermute | solution.py:20
  109.7 179.2 %all-gather.5.cloned.1.call-start = ((), (), s32[]{:S(2)}) async-start(), calls=%async_computation.4 | async-start | bytes 2359296 | tf_op jit(solution)/shard_map/all_gather | solution.py:101
  247.0 1.4 copy-start.1
  248.3 74.3 %reduce-scatter.5.cloned.1.call-start = ((), (), s32[]{:S(2)}) async-start(), calls=%async_computation.5 | async-start | bytes 1966080 | tf_op jit(solution)/shard_map/reduce_scatter | solution.py:113
Sparse Core Ops, SparseCore 0:
  26.2 31.6 all-gather.2
  109.9 132.5 reduce-scatter.2
  248.5 40.4 all-gather.4
  297.5 25.1 reduce-scatter.4
where the time goes:
time: 330 us; the launch traced here: 329 us
  waiting for transfers between devices  261 us (79%)
  blocking collectives  16.2 us (5%)
  matrix products  15.8 us (5%)
  other arithmetic  15.4 us (5%)
  between operations  13.2 us (4%)
  local copies, waits for them, and re-layouts  6.62 us (2%)
    reduce_scatter x1, waiting for transfers between devices, shards(): lax.psum_scatter(partial_value, 'mx', scatter_dimension=2, tiled=True)  132 us
    all_gather x1, waiting for transfers between devices, shards(): heads_rows = lax.all_gather(attended, 'mx', axis=1, tiled=True)  40.3 us
    all_gather x1, waiting for transfers between devices, shards(): own_rows = lax.all_gather(normed, 'my', axis=0, tiled=True)  31.7 us
    ppermute x1, waiting for transfers between devices, partner(): return lax.ppermute(block, axis, route)  31 us
    reduce_scatter x1, waiting for transfers between devices, shards(): lax.psum_scatter(jnp.dot(routed_rows, out_weight, preferred_element_type=...  25.3 us
    psum x1, blocking collectives, shards(): lax.psum((jnp.sum(values, axis=1), jnp.sum(values * values, axis=1)), 'mx')  16.2 us
    dot_general x1, matrix products, shards(): jnp.einsum('rd,dcf->rcf', packed, qkv_weight, preferred_element_type=jnp....  10.3 us
  transfers between devices with their start and end apart: 5, of which 5 were waited for; matrix products, arithmetic and copies ran while one was open for 1% of the time, Pallas kernels for 0%

commit v1 on v0

v1 whole, which is shorter than its diff:
```python
import jax
import jax.numpy as jnp
from jax import lax
from jax.experimental import pallas as pl
from jax.experimental.pallas import tpu as pltpu
from jax.sharding import PartitionSpec as P

D = 6144
HD = 128
BLK = 128
GRP = 8
R = 1024
SH = 256
DL = 768
CHIP = 2 * DL
IMG_ROWS = 512
ORDER = (0, 2, 1, 3)
F32 = jnp.float32
BF16 = jnp.bfloat16


def swap(block, axis, bits):
    count = lax.axis_size(axis)
    return lax.ppermute(block, axis, [(i, i ^ bits) for i in range(count)])


def shift(block, axis, step):
    count = lax.axis_size(axis)
    return lax.ppermute(block, axis, [((i + step) % count, i) for i in range(count)])


def weight_kernel(sibling, w_ref, keep_ref, send_ref, sems):
    mx = lax.axis_index("mx")
    z = mx >> 1
    lane = (mx & 1) ^ (1 if sibling else 0)
    copies = []
    for place, j in enumerate(ORDER):
        head = lane * 4 + (z ^ j)
        dst = keep_ref if place < 2 else send_ref
        for s in range(3):
            copies.append(
                pltpu.make_async_copy(
                    w_ref.at[s, :, pl.ds(pl.multiple_of(head * HD, HD), HD)],
                    dst.at[:, pl.ds((place % 2) * 3 * HD + s * HD, HD)],
                    sems.at[len(copies)],
                )
            )
    for copy in copies:
        copy.start()
    for copy in copies:
        copy.wait()


def weight_heads(w3, sibling):
    def kernel(w_ref, keep_ref, send_ref, sems):
        weight_kernel(sibling, w_ref, keep_ref, send_ref, sems)

    return pl.pallas_call(
        kernel,
        out_shape=[jax.ShapeDtypeStruct((DL, 6 * HD), BF16)] * 2,
        in_specs=[pl.BlockSpec(memory_space=pl.ANY)],
        out_specs=[pl.BlockSpec(memory_space=pl.ANY)] * 2,
        scratch_shapes=[pltpu.SemaphoreType.DMA((12,))],
        cost_estimate=pl.CostEstimate(flops=0, bytes_accessed=4 * DL * 6 * HD * 2, transcendentals=0),
    )(w3)


def out_weight_kernel(w_ref, out_ref, sems):
    mx = lax.axis_index("mx")
    z = mx >> 1
    copies = []
    for side in range(2):
        lane = (mx & 1) ^ side
        for j in range(4):
            head = lane * 4 + (z ^ j)
            copies.append(
                pltpu.make_async_copy(
                    w_ref.at[pl.ds(pl.multiple_of(head * HD, HD), HD), :],
                    out_ref.at[pl.ds((side * 4 + j) * HD, HD), :],
                    sems.at[len(copies)],
                )
            )
    for copy in copies:
        copy.start()
    for copy in copies:
        copy.wait()


def out_weight_heads(w):
    return pl.pallas_call(
        out_weight_kernel,
        out_shape=jax.ShapeDtypeStruct(w.shape, BF16),
        in_specs=[pl.BlockSpec(memory_space=pl.ANY)],
        out_specs=pl.BlockSpec(memory_space=pl.ANY),
        scratch_shapes=[pltpu.SemaphoreType.DMA((8,))],
        cost_estimate=pl.CostEstimate(flops=0, bytes_accessed=4 * R * DL, transcendentals=0),
    )(w)


def attention_kernel(counts_ref, coef_ref, cs_ref, *refs):
    own, got = refs[0:4], refs[4:8]
    out_ref, qkv = refs[8], refs[9]
    group = lax.axis_index("img")
    my = lax.axis_index("my")
    for k, offset in enumerate((0, 1, 3, 2)):
        coef = coef_ref[k * SH : (k + 1) * SH, :]
        total = own[k][...] + got[k][...].astype(F32)
        for c in range(4):
            total = total + coef[:, c + 1 : c + 2] * cs_ref[c : c + 1, :]
        total = total * coef[:, 0:1]
        shard = (my + offset) & 3
        qkv[pl.ds(pl.multiple_of(shard * SH, SH), SH), :] = total.astype(BF16)
    first = counts_ref[2 * group]
    second = counts_ref[2 * group + 1]
    for image in range(2):
        start = pl.multiple_of(first * BLK, BLK) if image else 0
        live = (second if image else first) * BLK
        q = qkv[pl.ds(start, IMG_ROWS), 0:HD]
        key = qkv[pl.ds(start, IMG_ROWS), HD : 2 * HD]
        value = qkv[pl.ds(start, IMG_ROWS), 2 * HD : 3 * HD]
        rows = lax.broadcasted_iota(jnp.int32, (IMG_ROWS, HD), 0)
        value = jnp.where(rows < live, value, jnp.zeros_like(value))
        scores = lax.dot_general(q, key, (((1,), (1,)), ((), ())), preferred_element_type=F32)
        columns = lax.broadcasted_iota(jnp.int32, (IMG_ROWS, IMG_ROWS), 1)
        scores = jnp.where(columns < live, scores * HD ** (-0.5), F32(-1e30))
        top = jnp.max(scores, axis=1, keepdims=True)
        powers = jnp.exp(scores - top)
        weights = (powers / jnp.sum(powers, axis=1, keepdims=True)).astype(BF16)
        mixture = jnp.dot(weights, value, preferred_element_type=F32)
        out_ref[image * IMG_ROWS : (image + 1) * IMG_ROWS, :] = mixture.astype(BF16)


def attention(counts, coef, cs, own, got):
    vmem = pl.BlockSpec(memory_space=pltpu.VMEM)
    return pl.pallas_call(
        attention_kernel,
        out_shape=jax.ShapeDtypeStruct((R, HD), BF16),
        in_specs=[pl.BlockSpec(memory_space=pltpu.SMEM)] + [vmem] * 10,
        out_specs=vmem,
        scratch_shapes=[pltpu.VMEM((R, 3 * HD), BF16)],
        compiler_params=pltpu.CompilerParams(vmem_limit_bytes=32 << 20),
        cost_estimate=pl.CostEstimate(
            flops=8 * IMG_ROWS * IMG_ROWS * HD, bytes_accessed=4 << 20, transcendentals=2 * IMG_ROWS * IMG_ROWS
        ),
    )(counts, coef, cs, *own, *got)


def route_kernel(counts_ref, owner_ref, target_ref, mine_ref, other_ref, far_ref, near_ref, source):
    group = lax.axis_index("img")
    my = lax.axis_index("my")
    for t in range(GRP):
        source[t] = -1
    base = (group >> 1) * 4
    offset = jnp.int32(0)
    for i in range(4):
        image = base + i
        count = counts_ref[image]
        owned = owner_ref[image] == group
        side = jnp.where((image >> 1) == group, 0, GRP)
        for b in range(4):

            @pl.when(owned & (b < count))
            def _():
                place = target_ref[0, jnp.minimum(offset + b, GRP - 1)]
                source[place] = side + (i & 1) * 4 + b

        offset = offset + jnp.where(owned, count, 0)
    for n, step in enumerate((2, 1, 3, 0)):
        shard = (my + step) & 3
        out_ref = far_ref if n < 2 else near_ref
        for half in range(2):
            src = source[2 * shard + half]
            place = pl.ds((n % 2) * SH + half * BLK, BLK)

            @pl.when(src < 0)
            def _():
                out_ref[place, :] = jnp.zeros((BLK, HD), BF16)

            @pl.when((src >= 0) & (src < GRP))
            def _():
                row = pl.multiple_of(jnp.clip(src, 0, GRP - 1) * BLK, BLK)
                out_ref[place, :] = mine_ref[pl.ds(row, BLK), :]

            @pl.when(src >= GRP)
            def _():
                row = pl.multiple_of(jnp.clip(src - GRP, 0, GRP - 1) * BLK, BLK)
                out_ref[place, :] = other_ref[pl.ds(row, BLK), :]


def route(counts, owner, target, mine, other):
    vmem = pl.BlockSpec(memory_space=pltpu.VMEM)
    smem = pl.BlockSpec(memory_space=pltpu.SMEM)
    return pl.pallas_call(
        route_kernel,
        out_shape=[jax.ShapeDtypeStruct((2 * SH, HD), BF16)] * 2,
        in_specs=[smem] * 3 + [vmem] * 2,
        out_specs=[vmem] * 2,
        scratch_shapes=[pltpu.SMEM((GRP,), jnp.int32)],
        cost_estimate=pl.CostEstimate(flops=0, bytes_accessed=R * HD * 4, transcendentals=0),
    )(counts, owner, target, mine, other)


def shards(patches, tile_counts, image_owner, block_target, qkv_weight, out_weight):
    rows = [patches, shift(patches, "my", 1), shift(patches, "my", -1), shift(patches, "my", 2)]
    w3 = jnp.transpose(qkv_weight, (1, 0, 2))
    theirs_keep, theirs_send = weight_heads(w3, True)
    sib_send = swap(theirs_send, "mx", 1)
    sib_keep = swap(theirs_keep, "mx", 1)
    own_keep, own_send = weight_heads(w3, False)
    wo = out_weight_heads(out_weight)

    ones = jnp.ones((8, DL), BF16)

    def total(a, b):
        return jnp.dot(ones, a, preferred_element_type=F32) + jnp.dot(ones, b, preferred_element_type=F32)

    cs_send = total(own_send, sib_send)
    cs_keep = total(own_keep, sib_keep)

    sums, squares, own, got = [], [], [], []
    for k in range(4):
        xo = rows[k]
        xs = swap(xo, "mx", 1)
        fo, fs = xo.astype(F32), xs.astype(F32)
        s1 = jnp.sum(fo, axis=1) + jnp.sum(fs, axis=1)
        s2 = jnp.sum(fo * fo, axis=1) + jnp.sum(fs * fs, axis=1)
        sums.append(s1)
        squares.append(s2)
        center = (s1 / CHIP)[:, None]
        part = (
            jnp.dot(xo, own_send, preferred_element_type=F32)
            + jnp.dot(xs, sib_send, preferred_element_type=F32)
            - center * cs_send[0:1, :]
        ).astype(BF16)
        first = swap(part, "mx", 2)
        kept = (
            jnp.dot(xo, own_keep, preferred_element_type=F32)
            + jnp.dot(xs, sib_keep, preferred_element_type=F32)
            - center * cs_keep[0:1, :]
        )
        mine = kept + first.astype(F32)
        second = swap(mine[:, 3 * HD :].astype(BF16), "mx", 4)
        own.append(mine[:, : 3 * HD])
        got.append(second)

    stats = jnp.stack(sums + squares, axis=0)
    w = 3 * HD
    cs = [cs_keep[:, :w], cs_send[:, :w], cs_keep[:, w:], cs_send[:, w:]]
    notes = [jnp.concatenate([stats, cs[0]], axis=1)]
    for j in (1, 2, 3):
        notes.append(swap(jnp.concatenate([stats, cs[j]], axis=1), "mx", 2 * j))
    all_stats = jnp.stack([n[:, :SH] for n in notes])
    chip_sum = all_stats[:, 0:4].reshape(4, R)
    chip_sq = all_stats[:, 4:8].reshape(4, R)
    mean = jnp.sum(chip_sum, axis=0) / D
    var = jnp.sum(chip_sq, axis=0) / D - mean * mean
    scale = lax.rsqrt(var + 1e-06)
    apart = chip_sum / CHIP - mean[None, :]
    coef = jnp.concatenate([scale[None, :], apart, jnp.zeros((3, R), F32)], axis=0).T
    cs_rows = jnp.concatenate([n[0:1, SH:] for n in notes], axis=0)

    attended = attention(tile_counts, coef, cs_rows, own, got)
    other = swap(attended, "img", 1)
    far, near = route(tile_counts, image_owner, block_target, attended, other)

    def project(block):
        lane = jnp.concatenate([block] + [swap(block, "mx", 2 * j) for j in (1, 2, 3)], axis=1)
        sib = swap(lane, "mx", 1)
        return jnp.dot(lane, wo[: 4 * HD], preferred_element_type=F32) + jnp.dot(
            sib, wo[4 * HD :], preferred_element_type=F32
        )

    far_out = project(far)
    near_out = project(near)
    from_far = shift(far_out[:SH].astype(BF16), "my", 2)
    from_up = shift(far_out[SH:].astype(BF16), "my", -1)
    from_down = shift(near_out[:SH].astype(BF16), "my", 1)
    out = near_out[SH:] + from_far.astype(F32) + from_up.astype(F32) + from_down.astype(F32)
    return out.astype(BF16)


def solution(mesh):
    in_specs = (
        P(("img", "my"), "mx"),
        P(),
        P(),
        P("img", None),
        P("mx", None, "my"),
        P("my", "mx"),
    )
    out_specs = P(("img", "my"), "mx")
    return jax.shard_map(shards, mesh=mesh, in_specs=in_specs, out_specs=out_specs, check_vma=False)
```

time: 330 us -> 364 us (1.10)
  Pallas kernels: 0 us -> 199 us
  waiting for transfers between devices: 261 us -> 85.5 us
  starting transfers between devices: 1.33 us -> 36.1 us
  blocking collectives: 16.2 us -> 0 us
  between operations: 13.2 us -> 0.77 us
  matrix products: 15.8 us -> 27.8 us
  other arithmetic: 15.4 us -> 5.21 us
    pallas_call x0 -> x5, Pallas kernels: none -> 199 us  [the longest x2 145 us: weight_heads(): pl.pallas_call(kernel, out_shape=[jax.ShapeDtypeStruct((DL, 6 * HD), BF16...]
    reduce_scatter x2 -> x0, waiting for transfers between devices: 157 us -> none  [the longest x1 132 us: shards(): lax.psum_scatter(partial_value, 'mx', scatter_dimension=2, tiled=True)]
    all_gather x2 -> x0, waiting for transfers between devices: 72.1 us -> none  [the longest x1 40.3 us: shards(): heads_rows = lax.all_gather(attended, 'mx', axis=1, tiled=True)]
    ppermute x1 -> x32, waiting for transfers between devices: 31 us -> 85.5 us  [the longest x26 69.7 us: swap(): return lax.ppermute(block, axis, [(i, i ^ bits) for i in range(count)])]
    ppermute x1 -> x32, starting transfers between devices: 1.21 us -> 36.1 us  [the longest x26 26.9 us: swap(): return lax.ppermute(block, axis, [(i, i ^ bits) for i in range(count)])]
    psum x1 -> x0, blocking collectives: 16.2 us -> none  [shards(): lax.psum((jnp.sum(values, axis=1), jnp.sum(values * values, axis=1)), 'mx')]
    dot_general x6 -> x24, matrix products: 15.8 us -> 27.8 us  [the longest x4 7.59 us: shards(): jnp.dot(xo, own_send, preferred_element_type=F32)]
    gather x2 -> x0, local copies, waits for them, and re-layouts: 6.1 us -> none  [the longest x1 3.56 us: shards(): jnp.take(heads_rows.reshape(BLK_GRP, BLK, feature_count), inverse, axis=0)]
  transfers between devices with their start and end apart: 5 -> 32, of which waited for: 5 -> 12; matrix products, arithmetic and copies ran while one was open for 1% -> 10% of each run, Pallas kernels for 0% -> 54%
where the time goes in v1:
time: 364 us; the launch traced here: 363 us
  Pallas kernels  199 us (55%)
  waiting for transfers between devices  85.5 us (23%)
  starting transfers between devices  36.1 us (10%)
  matrix products  27.8 us (8%)
  local copies, waits for them, and re-layouts  8.44 us (2%)
  other arithmetic  5.21 us (1%)
    pallas_call x2, Pallas kernels, weight_heads(): pl.pallas_call(kernel, out_shape=[jax.ShapeDtypeStruct((DL, 6 * HD), BF16...  145 us
    ppermute x26, waiting for transfers between devices, swap(): return lax.ppermute(block, axis, [(i, i ^ bits) for i in range(count)])  69.7 us
    pallas_call x1, Pallas kernels, out_weight_heads(): pl.pallas_call(out_weight_kernel, out_shape=jax.ShapeDtypeStruct(w.shape,...  48.8 us
    ppermute x26, starting transfers between devices, swap(): return lax.ppermute(block, axis, [(i, i ^ bits) for i in range(count)])  26.9 us
    ppermute x6, waiting for transfers between devices, shift(): lax.ppermute(block, axis, [((i + step) % count, i) for i in range(count)])  15.8 us
    ppermute x6, starting transfers between devices, shift(): lax.ppermute(block, axis, [((i + step) % count, i) for i in range(count)])  9.15 us
    dot_general x4, matrix products, shards(): jnp.dot(xo, own_send, preferred_element_type=F32)  7.59 us
    dot_general x4, matrix products, shards(): jnp.dot(xo, own_keep, preferred_element_type=F32)  7.5 us
  transfers between devices with their start and end apart: 32, of which 12 were waited for; matrix products, arithmetic and copies ran while one was open for 10% of the time, Pallas kernels for 54%

profile of v1, /device:TPU:1, one launch (start us, length us, event | category | flops | bytes accessed | tf_op | source)
XLA Modules:
  0.0 362.9 jit_solution(16864821920200180099)
XLA Ops:
  0.0 3.3 collective-permute-start.1
  6.6 72.7 %shard_map.65 = (bf16[768,768]{1,0:T(8,128)(2,1)}, bf16[768,768]{1,0:T(8,128)(2,1)}) custom-call(bf16[3,768,1024]{2,1,0:T(8,128)(2,1)} %bitcast.68), custom_call_target="tpu_custom_call" | custom-call | bytes 4718592 | tf_op jit(solution)/shard_map/pallas_call | solution.py:58
  79.4 72.7 %shard_map.64 = (bf16[768,768]{1,0:T(8,128)(2,1)}, bf16[768,768]{1,0:T(8,128)(2,1)}) custom-call(bf16[3,768,1024]{2,1,0:T(8,128)(2,1)} %bitcast.69), custom_call_target="tpu_custom_call" | custom-call | bytes 4718592 | tf_op jit(solution)/shard_map/pallas_call | solution.py:58
  162.1 2.4 fusion.50
  165.8 2.4 fusion.49
  168.2 2.4 fusion.48
  170.6 2.4 fusion.47
  180.4 4.4 %collective-permute-start.11 = (f32[8,640]{1,0:T(8,128)S(1)}, f32[8,640]{1,0:T(8,128)S(1)}, u32[]{:S(2)}, u32[]{:S(2)}) collective-permute-start(f32[8,640]{1,0:T(8,128)S(1)} %get-tuple-element.50), channel_id=1, source_target_pairs={{0,24},{4,28},{8,16},{12,20},{16,8},{20,12},{24,0},{28,4},{1,25},{... | collective-permute-start | bytes 61448 | tf_op jit(solution)/shard_map/ppermute | solution.py:24
  190.9 12.5 %collective-permute-done.10 = f32[8,640]{1,0:T(8,128)S(1)} collective-permute-done((f32[8,640]{1,0:T(8,128)S(1)}, f32[8,640]{1,0:T(8,128)S(1)}, u32[]{:S(2)}, u32[]{:S(2)}) %collective-permute-start.10) | collective-permute-done | bytes 20512 | tf_op jit(solution)/shard_map/ppermute | solution.py:24
  208.6 13.1 %collective-permute-done.13 = bf16[256,768]{1,0:T(8,128)(2,1)S(1)} collective-permute-done((bf16[256,768]{1,0:T(8,128)(2,1)S(1)}, bf16[256,768]{1,0:T(8,128)(2,1)S(1)}, u32[]{:S(2)}, u32[]{:S(2)}) %collective-permute-start.13) | collective-permute-done | bytes 393248 | tf_op jit(solution)/shard_map/ppermute | solution.py:24
  222.3 7.8 %collective-permute-done.12 = bf16[256,768]{1,0:T(8,128)(2,1)S(1)} collective-permute-done((bf16[256,768]{1,0:T(8,128)(2,1)S(1)}, bf16[256,768]{1,0:T(8,128)(2,1)S(1)}, u32[]{:S(2)}, u32[]{:S(2)}) %collective-permute-start.12) | collective-permute-done | bytes 393248 | tf_op jit(solution)/shard_map/ppermute | solution.py:24
  233.5 9.0 %collective-permute-done.17.refs_5_ = bf16[256,384]{1,0:T(8,128)(2,1)S(1)} collective-permute-done((bf16[256,384]{1,0:T(8,128)(2,1)S(1)}, bf16[256,384]{1,0:T(8,128)(2,1)S(1)}, u32[]{:S(2)}, u32[]{:S(2)}) %collective-permute-start.17) | collective-permute-done | bytes 196640 | tf_op jit(solution)/shard_map/ppermute | solution.py:24
  242.5 4.2 %collective-permute-done.16.refs_4_ = bf16[256,384]{1,0:T(8,128)(2,1)S(1)} collective-permute-done((bf16[256,384]{1,0:T(8,128)(2,1)}, bf16[256,384]{1,0:T(8,128)(2,1)S(1)}, u32[]{:S(2)}, u32[]{:S(2)}) %collective-permute-start.16) | collective-permute-done | bytes 196640 | tf_op jit(solution)/shard_map/ppermute | solution.py:24
  246.7 2.9 shard_map.66.mine_ref
  251.0 6.1 %collective-permute-done.20.other_ref = bf16[1024,128]{1,0:T(8,128)(2,1)S(1)} collective-permute-done((bf16[1024,128]{1,0:T(8,128)(2,1)S(1)}, bf16[1024,128]{1,0:T(8,128)(2,1)S(1)}, u32[]{:S(2)}, u32[]{:S(2)}) %collective-permute-start.20) | collective-permute-done | bytes 262176 | tf_op jit(solution)/shard_map/ppermute | solution.py:24
  260.4 3.0 collective-permute-start.26
  264.6 2.4 collective-permute-done.26
  267.0 4.3 %collective-permute-done.27 = bf16[512,128]{1,0:T(8,128)(2,1)S(1)} collective-permute-done((bf16[512,128]{1,0:T(8,128)(2,1)}, bf16[512,128]{1,0:T(8,128)(2,1)S(1)}, u32[]{:S(2)}, u32[]{:S(2)}) %collective-permute-start.27) | collective-permute-done | bytes 131104 | tf_op jit(solution)/shard_map/ppermute | solution.py:24
  271.4 3.9 %collective-permute-start.28 = (bf16[512,512]{1,0:T(8,128)(2,1)S(1)}, bf16[512,512]{1,0:T(8,128)(2,1)}, u32[]{:S(2)}, u32[]{:S(2)}) collective-permute-start(bf16[512,512]{1,0:T(8,128)(2,1)S(1)} %constant_dynamic-update-slice_fusion.4), channel_id=1, source_target_pairs={{0,4},{4,0},{8,12},{12,8},{16,20},{20,16},{24,28},{28,24},{1,5},{5... | collective-permute-start | bytes 1572872 | tf_op jit(solution)/shard_map/ppermute | solution.py:24
  277.0 48.8 %shard_map.68 = bf16[1024,768]{1,0:T(8,128)(2,1)} custom-call(bf16[1024,768]{1,0:T(8,128)(2,1)} %w_ref.1), custom_call_target="tpu_custom_call" | custom-call | bytes 3145728 | tf_op jit(solution)/shard_map/pallas_call | solution.py:90
  328.2 9.4 %collective-permute-done.22 = bf16[512,128]{1,0:T(8,128)(2,1)S(1)} collective-permute-done((bf16[512,128]{1,0:T(8,128)(2,1)S(1)}, bf16[512,128]{1,0:T(8,128)(2,1)S(1)}, u32[]{:S(2)}, u32[]{:S(2)}) %collective-permute-start.22) | collective-permute-done | bytes 131104 | tf_op jit(solution)/shard_map/ppermute | solution.py:24
  343.8 2.4 collective-permute-start.31
  346.2 6.9 %collective-permute-done.29 = bf16[256,768]{1,0:T(8,128)(2,1)S(1)} collective-permute-done((bf16[256,768]{1,0:T(8,128)(2,1)S(1)}, bf16[256,768]{1,0:T(8,128)(2,1)S(1)}, u32[]{:S(2)}, u32[]{:S(2)}) %collective-permute-start.29) | collective-permute-done | bytes 393248 | tf_op jit(solution)/shard_map/ppermute | solution.py:29
  353.1 8.9 %collective-permute-done.30 = bf16[256,768]{1,0:T(8,128)(2,1)S(1)} collective-permute-done((bf16[256,768]{1,0:T(8,128)(2,1)S(1)}, bf16[256,768]{1,0:T(8,128)(2,1)S(1)}, u32[]{:S(2)}, u32[]{:S(2)}) %collective-permute-start.30) | collective-permute-done | bytes 393248 | tf_op jit(solution)/shard_map/ppermute | solution.py:29
  (189 shorter events, 53.9 us)
Async XLA Ops:
  0.0 168.1 %collective-permute-start.1 = (bf16[256,768]{1,0:T(8,128)(2,1)}, bf16[256,768]{1,0:T(8,128)(2,1)}, u32[]{:S(2)}, u32[]{:S(2)}) collective-permute-start(bf16[256,768]{1,0:T(8,128)(2,1)} %param.6), channel_id=1, source_target_pairs={{1,0},{2,1},{3,2},{0,3},{5,4},{6,5},{7,6},{4,7},{9,8},{10,9},{11,1... | collective-permute-start | bytes 1179656 | tf_op jit(solution)/shard_map/ppermute | solution.py:29
  3.3 158.7 %collective-permute-start.3 = (bf16[256,768]{1,0:T(8,128)(2,1)}, bf16[256,768]{1,0:T(8,128)(2,1)}, u32[]{:S(2)}, u32[]{:S(2)}) collective-permute-start(bf16[256,768]{1,0:T(8,128)(2,1)} %param.6), channel_id=1, source_target_pairs={{3,0},{0,1},{1,2},{2,3},{7,4},{4,5},{5,6},{6,7},{11,8},{8,9},{9,10... | collective-permute-start | bytes 1179656 | tf_op jit(solution)/shard_map/ppermute | solution.py:29
  3.3 155.5 %collective-permute-start.5 = (bf16[256,768]{1,0:T(8,128)(2,1)}, bf16[256,768]{1,0:T(8,128)(2,1)S(1)}, u32[]{:S(2)}, u32[]{:S(2)}) collective-permute-start(bf16[256,768]{1,0:T(8,128)(2,1)} %param.6), channel_id=1, source_target_pairs={{2,0},{3,1},{0,2},{1,3},{6,4},{7,5},{4,6},{5,7},{10,8},{11,9},{8,1... | collective-permute-start | bytes 1179656 | tf_op jit(solution)/shard_map/ppermute | solution.py:29
  5.0 159.5 %collective-permute-start = (bf16[256,768]{1,0:T(8,128)(2,1)}, bf16[256,768]{1,0:T(8,128)(2,1)S(1)}, u32[]{:S(2)}, u32[]{:S(2)}) collective-permute-start(bf16[256,768]{1,0:T(8,128)(2,1)} %param.6), channel_id=1, source_target_pairs={{0,4},{4,0},{8,12},{12,8},{16,20},{20,16},{24,28},{28,24},{1,5},{5... | collective-permute-start | bytes 1179656 | tf_op jit(solution)/shard_map/ppermute | solution.py:24
  79.2 99.0 %collective-permute-start.7 = (bf16[768,768]{1,0:T(8,128)(2,1)}, bf16[768,768]{1,0:T(8,128)(2,1)S(1)}, u32[]{:S(2)}, u32[]{:S(2)}) collective-permute-start(bf16[768,768]{1,0:T(8,128)(2,1)} %get-tuple-element.12), channel_id=1, source_target_pairs={{0,4},{4,0},{8,12},{12,8},{16,20},{20,16},{24,28},{28,24},{1,5},{5... | collective-permute-start | bytes 3538952 | tf_op jit(solution)/shard_map/ppermute | solution.py:24
  158.8 20.5 %collective-permute-start.9 = (bf16[768,768]{1,0:T(8,128)(2,1)}, bf16[768,768]{1,0:T(8,128)(2,1)S(1)}, u32[]{:S(2)}, u32[]{:S(2)}) collective-permute-start(bf16[768,768]{1,0:T(8,128)(2,1)} %get-tuple-element.14), channel_id=1, source_target_pairs={{0,4},{4,0},{8,12},{12,8},{16,20},{20,16},{24,28},{28,24},{1,5},{5... | collective-permute-start | bytes 3538952 | tf_op jit(solution)/shard_map/ppermute | solution.py:24
  162.0 13.7 %collective-permute-start.4 = (bf16[256,768]{1,0:T(8,128)(2,1)}, bf16[256,768]{1,0:T(8,128)(2,1)S(1)}, u32[]{:S(2)}, u32[]{:S(2)}) collective-permute-start(bf16[256,768]{1,0:T(8,128)(2,1)} %collective-permute-done.3), channel_id=1, source_target_pairs={{0,4},{4,0},{8,12},{12,8},{16,20},{20,16},{24,28},{28,24},{1,5},{5... | collective-permute-start | bytes 1179656 | tf_op jit(solution)/shard_map/ppermute | solution.py:24
  164.5 12.0 %collective-permute-start.6 = (bf16[256,768]{1,0:T(8,128)(2,1)S(1)}, bf16[256,768]{1,0:T(8,128)(2,1)S(1)}, u32[]{:S(2)}, u32[]{:S(2)}) collective-permute-start(bf16[256,768]{1,0:T(8,128)(2,1)S(1)} %collective-permute-done.5), channel_id=1, source_target_pairs={{0,4},{4,0},{8,12},{12,8},{16,20},{20,16},{24,28},{28,24},{1,5},{5... | collective-permute-start | bytes 1179656 | tf_op jit(solution)/shard_map/ppermute | solution.py:24
  185.3 19.6 %collective-permute-start.15 = (bf16[256,768]{1,0:T(8,128)(2,1)S(1)}, bf16[256,768]{1,0:T(8,128)(2,1)S(1)}, u32[]{:S(2)}, u32[]{:S(2)}) collective-permute-start(bf16[256,768]{1,0:T(8,128)(2,1)S(1)} %fusion.15), channel_id=1, source_target_pairs={{0,8},{4,12},{8,0},{12,4},{16,24},{20,28},{24,16},{28,20},{1,9},{5... | collective-permute-start | bytes 1179656 | tf_op jit(solution)/shard_map/ppermute | solution.py:24
  186.5 20.5 %collective-permute-start.14 = (bf16[256,768]{1,0:T(8,128)(2,1)S(1)}, bf16[256,768]{1,0:T(8,128)(2,1)S(1)}, u32[]{:S(2)}, u32[]{:S(2)}) collective-permute-start(bf16[256,768]{1,0:T(8,128)(2,1)S(1)} %fusion.14), channel_id=1, source_target_pairs={{0,8},{4,12},{8,0},{12,4},{16,24},{20,28},{24,16},{28,20},{1,9},{5... | collective-permute-start | bytes 1179656 | tf_op jit(solution)/shard_map/ppermute | solution.py:24
  189.3 15.5 %collective-permute-start.8 = (f32[8,640]{1,0:T(8,128)S(1)}, f32[8,640]{1,0:T(8,128)S(1)}, u32[]{:S(2)}, u32[]{:S(2)}) collective-permute-start(f32[8,640]{1,0:T(8,128)S(1)} %get-tuple-element.48), channel_id=1, source_target_pairs={{0,8},{4,12},{8,0},{12,4},{16,24},{20,28},{24,16},{28,20},{1,9},{5... | collective-permute-start | bytes 61448 | tf_op jit(solution)/shard_map/ppermute | solution.py:24
  190.1 13.3 %collective-permute-start.10 = (f32[8,640]{1,0:T(8,128)S(1)}, f32[8,640]{1,0:T(8,128)S(1)}, u32[]{:S(2)}, u32[]{:S(2)}) collective-permute-start(f32[8,640]{1,0:T(8,128)S(1)} %get-tuple-element.49), channel_id=1, source_target_pairs={{0,16},{4,20},{8,24},{12,28},{16,0},{20,4},{24,8},{28,12},{1,17},{... | collective-permute-start | bytes 61448 | tf_op jit(solution)/shard_map/ppermute | solution.py:24
  190.1 31.6 %collective-permute-start.13 = (bf16[256,768]{1,0:T(8,128)(2,1)S(1)}, bf16[256,768]{1,0:T(8,128)(2,1)S(1)}, u32[]{:S(2)}, u32[]{:S(2)}) collective-permute-start(bf16[256,768]{1,0:T(8,128)(2,1)S(1)} %fusion.13), channel_id=1, source_target_pairs={{0,8},{4,12},{8,0},{12,4},{16,24},{20,28},{24,16},{28,20},{1,9},{5... | collective-permute-start | bytes 1179656 | tf_op jit(solution)/shard_map/ppermute | solution.py:24
  203.3 26.8 %collective-permute-start.12 = (bf16[256,768]{1,0:T(8,128)(2,1)S(1)}, bf16[256,768]{1,0:T(8,128)(2,1)S(1)}, u32[]{:S(2)}, u32[]{:S(2)}) collective-permute-start(bf16[256,768]{1,0:T(8,128)(2,1)S(1)} %fusion.12), channel_id=1, source_target_pairs={{0,8},{4,12},{8,0},{12,4},{16,24},{20,28},{24,16},{28,20},{1,9},{5... | collective-permute-start | bytes 1179656 | tf_op jit(solution)/shard_map/ppermute | solution.py:24
  205.5 28.1 %collective-permute-start.19 = (bf16[256,384]{1,0:T(8,128)(2,1)S(1)}, bf16[256,384]{1,0:T(8,128)(2,1)S(1)}, u32[]{:S(2)}, u32[]{:S(2)}) collective-permute-start(bf16[256,384]{1,0:T(8,128)(2,1)S(1)} %slice.186), channel_id=1, source_target_pairs={{0,16},{4,20},{8,24},{12,28},{16,0},{20,4},{24,8},{28,12},{1,17},{... | collective-permute-start | bytes 589832 | tf_op jit(solution)/shard_map/ppermute | solution.py:24
  207.5 26.0 %collective-permute-start.18 = (bf16[256,384]{1,0:T(8,128)(2,1)S(1)}, bf16[256,384]{1,0:T(8,128)(2,1)S(1)}, u32[]{:S(2)}, u32[]{:S(2)}) collective-permute-start(bf16[256,384]{1,0:T(8,128)(2,1)S(1)} %slice.187), channel_id=1, source_target_pairs={{0,16},{4,20},{8,24},{12,28},{16,0},{20,4},{24,8},{28,12},{1,17},{... | collective-permute-start | bytes 589832 | tf_op jit(solution)/shard_map/ppermute | solution.py:24
  222.2 20.3 %collective-permute-start.17 = (bf16[256,384]{1,0:T(8,128)(2,1)S(1)}, bf16[256,384]{1,0:T(8,128)(2,1)S(1)}, u32[]{:S(2)}, u32[]{:S(2)}) collective-permute-start(bf16[256,384]{1,0:T(8,128)(2,1)S(1)} %slice.188), channel_id=1, source_target_pairs={{0,16},{4,20},{8,24},{12,28},{16,0},{20,4},{24,8},{28,12},{1,17},{... | collective-permute-start | bytes 589832 | tf_op jit(solution)/shard_map/ppermute | solution.py:24
  231.4 15.3 %collective-permute-start.16 = (bf16[256,384]{1,0:T(8,128)(2,1)}, bf16[256,384]{1,0:T(8,128)(2,1)S(1)}, u32[]{:S(2)}, u32[]{:S(2)}) collective-permute-start(bf16[256,384]{1,0:T(8,128)(2,1)} %slice.189), channel_id=1, source_target_pairs={{0,16},{4,20},{8,24},{12,28},{16,0},{20,4},{24,8},{28,12},{1,17},{... | collective-permute-start | bytes 589832 | tf_op jit(solution)/shard_map/ppermute | solution.py:24
  271.4 67.0 %collective-permute-start.28 = (bf16[512,512]{1,0:T(8,128)(2,1)S(1)}, bf16[512,512]{1,0:T(8,128)(2,1)}, u32[]{:S(2)}, u32[]{:S(2)}) collective-permute-start(bf16[512,512]{1,0:T(8,128)(2,1)S(1)} %constant_dynamic-update-slice_fusion.4), channel_id=1, source_target_pairs={{0,4},{4,0},{8,12},{12,8},{16,20},{20,16},{24,28},{28,24},{1,5},{5... | collective-permute-start | bytes 1572872 | tf_op jit(solution)/shard_map/ppermute | solution.py:24
  275.3 52.9 %collective-permute-start.21 = (bf16[512,128]{1,0:T(8,128)(2,1)}, bf16[512,128]{1,0:T(8,128)(2,1)S(1)}, u32[]{:S(2)}, u32[]{:S(2)}) collective-permute-start(bf16[512,128]{1,0:T(8,128)(2,1)} %get-tuple-element.15), channel_id=1, source_target_pairs={{0,8},{4,12},{8,0},{12,4},{16,24},{20,28},{24,16},{28,20},{1,9},{5... | collective-permute-start | bytes 393224 | tf_op jit(solution)/shard_map/ppermute | solution.py:24
  325.9 11.7 %collective-permute-start.22 = (bf16[512,128]{1,0:T(8,128)(2,1)S(1)}, bf16[512,128]{1,0:T(8,128)(2,1)S(1)}, u32[]{:S(2)}, u32[]{:S(2)}) collective-permute-start(bf16[512,128]{1,0:T(8,128)(2,1)S(1)} %copy-done.28), channel_id=1, source_target_pairs={{0,16},{4,20},{8,24},{12,28},{16,0},{20,4},{24,8},{28,12},{1,17},{... | collective-permute-start | bytes 393224 | tf_op jit(solution)/shard_map/ppermute | solution.py:24
  340.9 12.2 %collective-permute-start.29 = (bf16[256,768]{1,0:T(8,128)(2,1)S(1)}, bf16[256,768]{1,0:T(8,128)(2,1)S(1)}, u32[]{:S(2)}, u32[]{:S(2)}) collective-permute-start(bf16[256,768]{1,0:T(8,128)(2,1)S(1)} %get-tuple-element.43), channel_id=1, source_target_pairs={{2,0},{3,1},{0,2},{1,3},{6,4},{7,5},{4,6},{5,7},{10,8},{11,9},{8,1... | collective-permute-start | bytes 1179656 | tf_op jit(solution)/shard_map/ppermute | solution.py:29
  342.0 20.0 %collective-permute-start.30 = (bf16[256,768]{1,0:T(8,128)(2,1)S(1)}, bf16[256,768]{1,0:T(8,128)(2,1)S(1)}, u32[]{:S(2)}, u32[]{:S(2)}) collective-permute-start(bf16[256,768]{1,0:T(8,128)(2,1)S(1)} %get-tuple-element.44), channel_id=1, source_target_pairs={{3,0},{0,1},{1,2},{2,3},{7,4},{4,5},{5,6},{6,7},{11,8},{8,9},{9,10... | collective-permute-start | bytes 1179656 | tf_op jit(solution)/shard_map/ppermute | solution.py:29
  343.8 18.2 %collective-permute-start.31 = (bf16[256,768]{1,0:T(8,128)(2,1)S(1)}, bf16[256,768]{1,0:T(8,128)(2,1)S(1)}, u32[]{:S(2)}, u32[]{:S(2)}) collective-permute-start(bf16[256,768]{1,0:T(8,128)(2,1)S(1)} %slice.185), channel_id=1, source_target_pairs={{1,0},{2,1},{3,2},{0,3},{5,4},{6,5},{7,6},{4,7},{9,8},{10,9},{11,1... | collective-permute-start | bytes 1179656 | tf_op jit(solution)/shard_map/ppermute | solution.py:29
  (38 other events, 387.2 us)

commit v2 on v0

v2 whole, which is shorter than its diff:
```python
import jax
import jax.numpy as jnp
from jax import lax
from jax.experimental import pallas as pl
from jax.experimental.pallas import tpu as pltpu
from jax.sharding import PartitionSpec as P

D = 6144
HD = 128
BLK = 128
GRP = 8
R = 1024
SH = 256
DL = 768
CHIP = 2 * DL
HEAD = 3 * HD
IMG_ROWS = 512
ORDER = (0, 2, 1, 3)
NOTE = R + HEAD
F32 = jnp.float32
BF16 = jnp.bfloat16

VMEM = pl.BlockSpec(memory_space=pltpu.VMEM)
SMEM = pl.BlockSpec(memory_space=pltpu.SMEM)
ANY = pl.BlockSpec(memory_space=pl.ANY)


def call(kernel, outs, ins, scratch=(), flops=0, moved=1 << 20, exps=0, limit=16, out_specs=None):
    out_shape = [jax.ShapeDtypeStruct(s, d) for s, d in outs]
    return pl.pallas_call(
        kernel,
        out_shape=out_shape,
        in_specs=ins,
        out_specs=out_specs or [VMEM] * len(outs),
        scratch_shapes=list(scratch),
        compiler_params=pltpu.CompilerParams(vmem_limit_bytes=limit << 20),
        cost_estimate=pl.CostEstimate(flops=flops, bytes_accessed=moved, transcendentals=exps),
    )


def swap(block, axis, bits):
    count = lax.axis_size(axis)
    return lax.ppermute(block, axis, [(i, i ^ bits) for i in range(count)])


def shift(block, axis, step):
    count = lax.axis_size(axis)
    return lax.ppermute(block, axis, [((i + step) % count, i) for i in range(count)])


def weight_heads(w3, sibling):
    def kernel(w_ref, keep_ref, send_ref, sems):
        mx = lax.axis_index("mx")
        z = mx >> 1
        lane = (mx & 1) ^ (1 if sibling else 0)
        copies = []
        for place in (2, 3, 0, 1):
            head = lane * 4 + (z ^ ORDER[place])
            dst = keep_ref if place < 2 else send_ref
            for s in range(3):
                copies.append(
                    pltpu.make_async_copy(
                        w_ref.at[s, :, pl.ds(pl.multiple_of(head * HD, HD), HD)],
                        dst.at[:, pl.ds((place % 2) * HEAD + s * HD, HD)],
                        sems.at[len(copies)],
                    )
                )
        for copy in copies:
            copy.start()
        for copy in copies:
            copy.wait()

    shape = ((DL, 2 * HEAD), BF16)
    return call(kernel, [shape, shape], [ANY], [pltpu.SemaphoreType.DMA((12,))], moved=8 * DL * HEAD)(w3)


def out_weight_heads(w):
    def kernel(w_ref, out_ref, sems):
        mx = lax.axis_index("mx")
        z = mx >> 1
        copies = []
        for side in range(2):
            lane = (mx & 1) ^ side
            for j in range(4):
                head = lane * 4 + (z ^ j)
                copies.append(
                    pltpu.make_async_copy(
                        w_ref.at[pl.ds(pl.multiple_of(head * HD, HD), HD), :],
                        out_ref.at[pl.ds((side * 4 + j) * HD, HD), :],
                        sems.at[len(copies)],
                    )
                )
        for copy in copies:
            copy.start()
        for copy in copies:
            copy.wait()

    (out,) = call(kernel, [(w.shape, BF16)], [ANY], [pltpu.SemaphoreType.DMA((8,))], moved=4 * R * DL)(w)
    return out


def table(counts, owner, target):
    def kernel(counts_ref, owner_ref, target_ref, out_ref, source):
        group = lax.axis_index("img")
        my = lax.axis_index("my")
        for t in range(GRP):
            source[t] = -1
        base = (group >> 1) * 4
        offset = jnp.int32(0)
        for i in range(4):
            image = base + i
            count = counts_ref[image]
            owned = owner_ref[image] == group
            side = jnp.where((image >> 1) == group, 0, GRP)
            for b in range(4):

                @pl.when(owned & (b < count))
                def _():
                    place = target_ref[0, jnp.minimum(offset + b, GRP - 1)]
                    source[place] = side + (i & 1) * 4 + b

            offset = offset + jnp.where(owned, count, 0)
        for n, step in enumerate((2, 1, 3, 0)):
            shard = (my + step) & 3
            out_ref[2 * n] = source[2 * shard]
            out_ref[2 * n + 1] = source[2 * shard + 1]
        out_ref[8] = counts_ref[2 * group]
        out_ref[9] = counts_ref[2 * group + 1]

    (out,) = call(
        kernel,
        [((16,), jnp.int32)],
        [SMEM] * 3,
        [pltpu.SMEM((GRP,), jnp.int32)],
        moved=1 << 10,
        limit=4,
        out_specs=[SMEM],
    )(counts, owner, target)
    return out


def load_rows(rows, xo_ref, xs_ref):
    rows[0:SH, 0:DL] = xo_ref[...]
    rows[0:SH, DL:CHIP] = xs_ref[...]
    rows[SH : SH + 16, :] = jnp.ones((16, CHIP), BF16)


def row_stats(xo_ref, xs_ref):
    fo, fs = xo_ref[...].astype(F32), xs_ref[...].astype(F32)
    s1 = jnp.sum(fo, axis=1, keepdims=True) + jnp.sum(fs, axis=1, keepdims=True)
    s2 = jnp.sum(fo * fo, axis=1, keepdims=True) + jnp.sum(fs * fs, axis=1, keepdims=True)
    lane = lax.broadcasted_iota(jnp.int32, (SH, HD), 1)
    return jnp.where(lane == 0, s1, jnp.where(lane == 1, s2, F32(0.0)))


def partial_tile(rows, wo_ref, ws_ref, columns, center):
    acc = jnp.dot(rows[:, 0:DL], wo_ref[:, columns], preferred_element_type=F32)
    acc = acc + jnp.dot(rows[:, DL:CHIP], ws_ref[:, columns], preferred_element_type=F32)
    sums = acc[SH : SH + 8, :]
    return acc[0:SH, :] - center * sums[0:1, :], sums


ROWS_SCRATCH = pltpu.VMEM((SH + 16, CHIP), BF16)
PART_FLOPS = 2 * SH * CHIP * 2 * HEAD


def send_part(xo, xs, wo, ws):
    def kernel(xo_ref, xs_ref, wo_ref, ws_ref, out_ref, stat_ref, rows):
        load_rows(rows, xo_ref, xs_ref)
        stat = row_stats(xo_ref, xs_ref)
        stat_ref[...] = stat
        center = stat[:, 0:1] / CHIP
        for n in range(3):
            columns = slice(n * 256, (n + 1) * 256)
            tile, _ = partial_tile(rows, wo_ref, ws_ref, columns, center)
            out_ref[:, columns] = tile.astype(BF16)

    return call(
        kernel, [((SH, 2 * HEAD), BF16), ((SH, HD), F32)], [VMEM] * 4, [ROWS_SCRATCH], PART_FLOPS
    )(xo, xs, wo, ws)


def keep_part(xo, xs, wo, ws, stat, got):
    def kernel(xo_ref, xs_ref, wo_ref, ws_ref, stat_ref, got_ref, own_ref, send_ref, rows):
        load_rows(rows, xo_ref, xs_ref)
        center = stat_ref[:, 0:1] / CHIP
        for n in range(6):
            columns = slice(n * HD, (n + 1) * HD)
            if n % 2 == 0:
                pair, _ = partial_tile(rows, wo_ref, ws_ref, slice(n * HD, (n + 2) * HD), center)
            tile = pair[:, (n % 2) * HD : (n % 2 + 1) * HD] + got_ref[:, columns].astype(F32)
            if n < 3:
                own_ref[:, columns] = tile
            else:
                send_ref[:, (n - 3) * HD : (n - 2) * HD] = tile.astype(BF16)

    return call(
        kernel, [((SH, HEAD), F32), ((SH, HEAD), BF16)], [VMEM] * 6, [ROWS_SCRATCH], PART_FLOPS
    )(xo, xs, wo, ws, stat, got)


def whole_part(xo, xs, weights, stats):
    def kernel(xo_ref, xs_ref, ko_ref, ks_ref, so_ref, ss_ref, t0_ref, t1_ref, t2_ref, *refs):
        own_ref, p1_ref, p2_ref, p3_ref = refs[0:4]
        notes, rows = refs[4:8], refs[8]
        load_rows(rows, xo_ref, xs_ref)
        stat = row_stats(xo_ref, xs_ref)
        center = stat[:, 0:1] / CHIP
        for wo_ref, ws_ref, outs, js in ((so_ref, ss_ref, (p1_ref, p3_ref), (1, 3)), (ko_ref, ks_ref, (own_ref, p2_ref), (0, 2))):
            for n in range(6):
                if n % 2 == 0:
                    pair, sums = partial_tile(rows, wo_ref, ws_ref, slice(n * HD, (n + 2) * HD), center)
                half = slice((n % 2) * HD, (n % 2 + 1) * HD)
                columns = slice((n % 3) * HD, (n % 3 + 1) * HD)
                out_ref = outs[n // 3]
                out_ref[:, columns] = pair[:, half].astype(out_ref.dtype)
                notes[js[n // 3]][:, R + (n % 3) * HD : R + (n % 3 + 1) * HD] = sums[:, half]
        for k, one in enumerate((t0_ref[...], t1_ref[...], t2_ref[...], stat)):
            turned = one.T[0:8, :]
            for note in notes:
                note[:, k * SH : (k + 1) * SH] = turned

    part = ((SH, HEAD), BF16)
    note = ((8, NOTE), F32)
    return call(
        kernel, [((SH, HEAD), F32), part, part, part] + [note] * 4, [VMEM] * 9, [ROWS_SCRATCH], 2 * PART_FLOPS
    )(xo, xs, *weights, *stats)


def coefficients(notes):
    def kernel(n0_ref, n1_ref, n2_ref, n3_ref, coef_ref, cs_ref):
        refs = (n0_ref, n1_ref, n2_ref, n3_ref)
        sums = [n[0:1, 0:R] for n in refs]
        mean = (sums[0] + sums[1] + sums[2] + sums[3]) / D
        squares = n0_ref[1:2, 0:R] + n1_ref[1:2, 0:R] + n2_ref[1:2, 0:R] + n3_ref[1:2, 0:R]
        var = squares / D - mean * mean
        scale = lax.rsqrt(var + 1e-06)
        lines = [scale] + [s / CHIP - mean for s in sums] + [jnp.zeros((HD - 5, R), F32)]
        coef_ref[...] = jnp.concatenate(lines, axis=0).T
        for c, n in enumerate(refs):
            cs_ref[c : c + 1, :] = n[0:1, R:NOTE]
        cs_ref[4:8, :] = jnp.zeros((4, HEAD), F32)

    return call(kernel, [((R, HD), F32), ((8, HEAD), F32)], [VMEM] * 4)(*notes)


def attention(places, coef, cs, parts):
    flat = [p for chunk in parts for p in chunk]

    def kernel(places_ref, coef_ref, cs_ref, *refs):
        out_ref, qkv = refs[len(flat)], refs[len(flat) + 1]
        my = lax.axis_index("my")
        at = 0
        for k, offset in enumerate((0, 1, 3, 2)):
            coef = coef_ref[k * SH : (k + 1) * SH, :]
            total = refs[at][...]
            for more in range(1, len(parts[k])):
                total = total + refs[at + more][...].astype(F32)
            at += len(parts[k])
            for c in range(4):
                total = total + coef[:, c + 1 : c + 2] * cs_ref[c : c + 1, :]
            total = total * coef[:, 0:1]
            shard = (my + offset) & 3
            qkv[pl.ds(pl.multiple_of(shard * SH, SH), SH), :] = total.astype(BF16)
        first, second = places_ref[8], places_ref[9]
        for image in range(2):
            start = pl.multiple_of(first * BLK, BLK) if image else 0
            live = (second if image else first) * BLK
            q = qkv[pl.ds(start, IMG_ROWS), 0:HD]
            key = qkv[pl.ds(start, IMG_ROWS), HD : 2 * HD]
            value = qkv[pl.ds(start, IMG_ROWS), 2 * HD : 3 * HD]
            rows = lax.broadcasted_iota(jnp.int32, (IMG_ROWS, HD), 0)
            value = jnp.where(rows < live, value, jnp.zeros_like(value))
            scores = lax.dot_general(q, key, (((1,), (1,)), ((), ())), preferred_element_type=F32)
            columns = lax.broadcasted_iota(jnp.int32, (IMG_ROWS, IMG_ROWS), 1)
            scores = jnp.where(columns < live, scores * HD ** (-0.5), F32(-1e30))
            top = jnp.max(scores, axis=1, keepdims=True)
            powers = jnp.exp(scores - top)
            weights = (powers / jnp.sum(powers, axis=1, keepdims=True)).astype(BF16)
            mixture = jnp.dot(weights, value, preferred_element_type=F32)
            out_ref[image * IMG_ROWS : (image + 1) * IMG_ROWS, :] = mixture.astype(BF16)

    (out,) = call(
        kernel,
        [((R, HD), BF16)],
        [SMEM] + [VMEM] * (2 + len(flat)),
        [pltpu.VMEM((R, HEAD), BF16)],
        8 * IMG_ROWS * IMG_ROWS * HD,
        4 << 20,
        2 * IMG_ROWS * IMG_ROWS,
        24,
    )(places, coef, cs, *flat)
    return out


def route(places, mine, other):
    def kernel(places_ref, mine_ref, other_ref, *outs):
        for n in range(GRP):
            out_ref, at = ((outs[0], 0), (outs[1], 2), (outs[2], 6))[(0, 0, 1, 1, 1, 1, 2, 2)[n]]
            place = slice((n - at) * BLK, (n - at + 1) * BLK)
            src = places_ref[n]
            row = pl.multiple_of((src & 7) * BLK, BLK)

            @pl.when(src < 0)
            def _():
                out_ref[place, :] = jnp.zeros((BLK, HD), BF16)

            @pl.when((src >= 0) & (src < GRP))
            def _():
                out_ref[place, :] = mine_ref[pl.ds(row, BLK), :]

            @pl.when(src >= GRP)
            def _():
                out_ref[place, :] = other_ref[pl.ds(row, BLK), :]

    outs = [((SH, HD), BF16), ((2 * SH, HD), BF16), ((SH, HD), BF16)]
    return call(kernel, outs, [SMEM, VMEM, VMEM])(places, mine, other)


def project(block, wo, dtype):
    lane = [block] + [swap(block, "mx", 2 * j) for j in (1, 2, 3)]
    heads = lane + [swap(one, "mx", 1) for one in lane]
    count = block.shape[0] // SH

    def kernel(*refs):
        w_ref, outs, rows = refs[8], refs[9 : 9 + count], refs[9 + count]
        for h in range(8):
            rows[:, h * HD : (h + 1) * HD] = refs[h][...]
        for i, out_ref in enumerate(outs):
            for n in range(3):
                columns = slice(n * 256, (n + 1) * 256)
                tile = jnp.dot(rows[i * SH : (i + 1) * SH, :], w_ref[:, columns], preferred_element_type=F32)
                out_ref[:, columns] = tile.astype(out_ref.dtype)

    return call(
        kernel,
        [((SH, DL), dtype)] * count,
        [VMEM] * 9,
        [pltpu.VMEM((count * SH, R), BF16)],
        2 * count * SH * R * DL,
    )(*heads, wo)


def shards(patches, tile_counts, image_owner, block_target, qkv_weight, out_weight):
    rows = [patches, shift(patches, "my", 1), shift(patches, "my", -1), shift(patches, "my", 2)]
    w3 = jnp.transpose(qkv_weight, (1, 0, 2))
    theirs_keep, theirs_send = weight_heads(w3, True)
    sib_send = swap(theirs_send, "mx", 1)
    sib_keep = swap(theirs_keep, "mx", 1)
    own_keep, own_send = weight_heads(w3, False)
    wo = out_weight_heads(out_weight)
    places = table(tile_counts, image_owner, block_target)
    sibs = [swap(x, "mx", 1) for x in rows]

    parts, stats = [], []
    for k in range(3):
        part, stat = send_part(rows[k], sibs[k], own_send, sib_send)
        stats.append(stat)
        got = swap(part, "mx", 2)
        own, second = keep_part(rows[k], sibs[k], own_keep, sib_keep, stat, got)
        parts.append((own, swap(second, "mx", 4)))
    weights = (own_keep, sib_keep, own_send, sib_send)
    own, p1, p2, p3, n0, n1, n2, n3 = whole_part(rows[3], sibs[3], weights, stats)
    parts.append((own, swap(p2, "mx", 4), swap(p3, "mx", 6), swap(p1, "mx", 2)))
    coef, cs = coefficients([n0, swap(n1, "mx", 2), swap(n2, "mx", 4), swap(n3, "mx", 6)])

    attended = attention(places, coef, cs, parts)
    other = swap(attended, "img", 1)
    across, beside, here = route(places, attended, other)

    (far,) = project(across, wo, BF16)
    up, down = project(beside, wo, BF16)
    (mine,) = project(here, wo, F32)
    from_far = shift(far, "my", 2)
    from_up = shift(up, "my", -1)
    from_down = shift(down, "my", 1)
    out = mine + from_far.astype(F32) + from_up.astype(F32) + from_down.astype(F32)
    return out.astype(BF16)


def solution(mesh):
    in_specs = (
        P(("img", "my"), "mx"),
        P(),
        P(),
        P("img", None),
        P("mx", None, "my"),
        P("my", "mx"),
    )
    out_specs = P(("img", "my"), "mx")
    return jax.shard_map(shards, mesh=mesh, in_specs=in_specs, out_specs=out_specs, check_vma=False)
```

time: 330 us -> 167 us (0.51)
  waiting for transfers between devices: 261 us -> 76.5 us
  starting transfers between devices: 1.33 us -> 65.5 us
  Pallas kernels: 0 us -> 18.2 us
  blocking collectives: 16.2 us -> 0 us
  matrix products: 15.8 us -> 0 us
  other arithmetic: 15.4 us -> 0.95 us
  between operations: 13.2 us -> 0.47 us
  local copies, waits for them, and re-layouts: 6.62 us -> 2.35 us
    reduce_scatter x2 -> x0, waiting for transfers between devices: 157 us -> none  [the longest x1 132 us: shards(): lax.psum_scatter(partial_value, 'mx', scatter_dimension=2, tiled=True)]
    all_gather x2 -> x0, waiting for transfers between devices: 72.1 us -> none  [the longest x1 40.3 us: shards(): heads_rows = lax.all_gather(attended, 'mx', axis=1, tiled=True)]
    ppermute x1 -> x46, starting transfers between devices: 1.21 us -> 65.5 us  [the longest x40 58.4 us: swap(): return lax.ppermute(block, axis, [(i, i ^ bits) for i in range(count)])]
    ppermute x1 -> x46, waiting for transfers between devices: 31 us -> 76.5 us  [the longest x40 57.1 us: swap(): return lax.ppermute(block, axis, [(i, i ^ bits) for i in range(count)])]
    pallas_call x0 -> x17, Pallas kernels: none -> 18.2 us  [the longest x3 3 us: send_part(): call(kernel, [((SH, 2 * HEAD), BF16), ((SH, HD), F32)], [VMEM] * 4, [ROWS...]
    psum x1 -> x0, blocking collectives: 16.2 us -> none  [shards(): lax.psum((jnp.sum(values, axis=1), jnp.sum(values * values, axis=1)), 'mx')]
    dot_general x6 -> x0, matrix products: 15.8 us -> none  [the longest x1 10.3 us: shards(): jnp.einsum('rd,dcf->rcf', packed, qkv_weight, preferred_element_type=jnp....]
    gather x2 -> x0, local copies, waits for them, and re-layouts: 6.1 us -> none  [the longest x1 3.56 us: shards(): jnp.take(heads_rows.reshape(BLK_GRP, BLK, feature_count), inverse, axis=0)]
  transfers between devices with their start and end apart: 5 -> 46, of which waited for: 5 -> 17; matrix products, arithmetic and copies ran while one was open for 1% -> 0% of each run, Pallas kernels for 0% -> 8%
where the time goes in v2:
time: 167 us; the launch traced here: 164 us
  waiting for transfers between devices  76.5 us (46%)
  starting transfers between devices  65.5 us (39%)
  Pallas kernels  18.2 us (11%)
  local copies, waits for them, and re-layouts  2.35 us (1%)
    ppermute x40, starting transfers between devices, swap(): return lax.ppermute(block, axis, [(i, i ^ bits) for i in range(count)])  58.4 us
    ppermute x40, waiting for transfers between devices, swap(): return lax.ppermute(block, axis, [(i, i ^ bits) for i in range(count)])  57.1 us
    ppermute x6, waiting for transfers between devices, shift(): lax.ppermute(block, axis, [((i + step) % count, i) for i in range(count)])  19.3 us
    ppermute x6, starting transfers between devices, shift(): lax.ppermute(block, axis, [((i + step) % count, i) for i in range(count)])  7.09 us
  transfers between devices with their start and end apart: 46, of which 17 were waited for; matrix products, arithmetic and copies ran while one was open for 0% of the time, Pallas kernels for 8%

profile of v2, /device:TPU:1, one launch (start us, length us, event | category | flops | bytes accessed | tf_op | source)
XLA Modules:
  0.0 163.9 jit_solution(18406998412856423797)
XLA Ops:
  0.0 2.3 %copy-done = bf16[768,3,1024]{2,0,1:T(8,128)(2,1)S(1)} copy-done((bf16[768,3,1024]{2,0,1:T(8,128)(2,1)S(1)}, bf16[768,3,1024]{2,0,1:T(8,128)(2,1)}, u32[]{:S(2)}) %copy-start) | copy-done | bytes 4718616
  3.1 3.3 %collective-permute-start.3 = (bf16[768,768]{1,0:T(8,128)(2,1)S(1)}, bf16[768,768]{1,0:T(8,128)(2,1)S(1)}, u32[]{:S(2)}, u32[]{:S(2)}) collective-permute-start(bf16[768,768]{1,0:T(8,128)(2,1)S(1)} %get-tuple-element.39), channel_id=1, source_target_pairs={{0,4},{4,0},{8,12},{12,8},{16,20},{20,16},{24,28},{28,24},{1,5},{5... | collective-permute-start | bytes 3538952 | tf_op jit(solution)/shard_map/ppermute | solution.py:43
  6.6 2.9 %collective-permute-start.5 = (bf16[256,768]{1,0:T(8,128)(2,1)S(1)}, bf16[256,768]{1,0:T(8,128)(2,1)S(1)}, u32[]{:S(2)}, u32[]{:S(2)}) collective-permute-start(bf16[256,768]{1,0:T(8,128)(2,1)S(1)} %copy-done.1), channel_id=1, source_target_pairs={{1,0},{2,1},{3,2},{0,3},{5,4},{6,5},{7,6},{4,7},{9,8},{10,9},{11,1... | collective-permute-start | bytes 1179656 | tf_op jit(solution)/shard_map/ppermute | solution.py:48
  9.5 17.1 %collective-permute-done.7.xo_ref = bf16[256,768]{1,0:T(8,128)(2,1)S(1)} collective-permute-done((bf16[256,768]{1,0:T(8,128)(2,1)S(1)}, bf16[256,768]{1,0:T(8,128)(2,1)S(1)}, u32[]{:S(2)}, u32[]{:S(2)}) %collective-permute-start.7) | collective-permute-done | bytes 393248 | tf_op jit(solution)/shard_map/ppermute | solution.py:48
  36.8 2.2 %collective-permute-start.18 = (bf16[256,384]{1,0:T(8,128)(2,1)S(1)}, bf16[256,384]{1,0:T(8,128)(2,1)S(1)}, u32[]{:S(2)}, u32[]{:S(2)}) collective-permute-start(bf16[256,384]{1,0:T(8,128)(2,1)S(1)} %get-tuple-element.59), channel_id=1, source_target_pairs={{0,16},{4,20},{8,24},{12,28},{16,0},{20,4},{24,8},{28,12},{1,17},{... | collective-permute-start | bytes 589832 | tf_op jit(solution)/shard_map/ppermute | solution.py:43
  39.2 7.7 %collective-permute-done.16.got_ref = bf16[256,768]{1,0:T(8,128)(2,1)S(1)} collective-permute-done((bf16[256,768]{1,0:T(8,128)(2,1)S(1)}, bf16[256,768]{1,0:T(8,128)(2,1)S(1)}, u32[]{:S(2)}, u32[]{:S(2)}) %collective-permute-start.16) | collective-permute-done | bytes 393248 | tf_op jit(solution)/shard_map/ppermute | solution.py:43
  49.4 6.0 %collective-permute-done.14.got_ref = bf16[256,768]{1,0:T(8,128)(2,1)S(1)} collective-permute-done((bf16[256,768]{1,0:T(8,128)(2,1)S(1)}, bf16[256,768]{1,0:T(8,128)(2,1)S(1)}, u32[]{:S(2)}, u32[]{:S(2)}) %collective-permute-start.14) | collective-permute-done | bytes 393248 | tf_op jit(solution)/shard_map/ppermute | solution.py:43
  56.3 7.5 %collective-permute-done.12.got_ref = bf16[256,768]{1,0:T(8,128)(2,1)S(1)} collective-permute-done((bf16[256,768]{1,0:T(8,128)(2,1)S(1)}, bf16[256,768]{1,0:T(8,128)(2,1)S(1)}, u32[]{:S(2)}, u32[]{:S(2)}) %collective-permute-start.12) | collective-permute-done | bytes 393248 | tf_op jit(solution)/shard_map/ppermute | solution.py:43
  66.3 2.0 %collective-permute-start.17 = (bf16[256,384]{1,0:T(8,128)(2,1)S(1)}, bf16[256,384]{1,0:T(8,128)(2,1)S(1)}, u32[]{:S(2)}, u32[]{:S(2)}) collective-permute-start(bf16[256,384]{1,0:T(8,128)(2,1)S(1)} %get-tuple-element.57), channel_id=1, source_target_pairs={{0,16},{4,20},{8,24},{12,28},{16,0},{20,4},{24,8},{28,12},{1,17},{... | collective-permute-start | bytes 589832 | tf_op jit(solution)/shard_map/ppermute | solution.py:43
  68.8 2.0 %collective-permute-start.13 = (bf16[256,384]{1,0:T(8,128)(2,1)S(1)}, bf16[256,384]{1,0:T(8,128)(2,1)S(1)}, u32[]{:S(2)}, u32[]{:S(2)}) collective-permute-start(bf16[256,384]{1,0:T(8,128)(2,1)S(1)} %get-tuple-element.51), channel_id=1, source_target_pairs={{0,16},{4,20},{8,24},{12,28},{16,0},{20,4},{24,8},{28,12},{1,17},{... | collective-permute-start | bytes 589832 | tf_op jit(solution)/shard_map/ppermute | solution.py:43
  72.2 5.7 %collective-permute-done.20.refs_9_ = bf16[256,384]{1,0:T(8,128)(2,1)S(1)} collective-permute-done((bf16[256,384]{1,0:T(8,128)(2,1)S(1)}, bf16[256,384]{1,0:T(8,128)(2,1)S(1)}, u32[]{:S(2)}, u32[]{:S(2)}) %collective-permute-start.20) | collective-permute-done | bytes 196640 | tf_op jit(solution)/shard_map/ppermute | solution.py:43
  78.0 11.5 %collective-permute-done.17.refs_5_ = bf16[256,384]{1,0:T(8,128)(2,1)S(1)} collective-permute-done((bf16[256,384]{1,0:T(8,128)(2,1)S(1)}, bf16[256,384]{1,0:T(8,128)(2,1)S(1)}, u32[]{:S(2)}, u32[]{:S(2)}) %collective-permute-start.17) | collective-permute-done | bytes 196640 | tf_op jit(solution)/shard_map/ppermute | solution.py:43
  89.5 4.2 %collective-permute-done.15.refs_3_ = bf16[256,384]{1,0:T(8,128)(2,1)S(1)} collective-permute-done((bf16[256,384]{1,0:T(8,128)(2,1)S(1)}, bf16[256,384]{1,0:T(8,128)(2,1)S(1)}, u32[]{:S(2)}, u32[]{:S(2)}) %collective-permute-start.15) | collective-permute-done | bytes 196640 | tf_op jit(solution)/shard_map/ppermute | solution.py:43
  93.7 4.2 %collective-permute-done.13.refs_1_ = bf16[256,384]{1,0:T(8,128)(2,1)S(1)} collective-permute-done((bf16[256,384]{1,0:T(8,128)(2,1)S(1)}, bf16[256,384]{1,0:T(8,128)(2,1)S(1)}, u32[]{:S(2)}, u32[]{:S(2)}) %collective-permute-start.13) | collective-permute-done | bytes 196640 | tf_op jit(solution)/shard_map/ppermute | solution.py:43
  97.9 3.0 %shard_map.75.mine_ref = bf16[1024,128]{1,0:T(8,128)(2,1)S(1)} custom-call(s32[16]{0:T(128)S(1)} %shard_map.64.places_ref, f32[1024,128]{1,0:T(8,128)S(1)} %get-tuple-element.47.coef_ref, f32[8,384]{1,0:T(8,128)S(1)} %get-tuple-element.48.cs_ref, f32[256,384]{1,0:T(8,128)S(1)} %get-tuple-element.50.refs_0_, ...), custom_call_target="tpu_custom_call" | custom-call | flops 268435456 | bytes 4194304 | tf_op jit(solution)/shard_map/pallas_call | solution.py:283
  102.3 4.2 %collective-permute-done.21.other_ref = bf16[1024,128]{1,0:T(8,128)(2,1)S(1)} collective-permute-done((bf16[1024,128]{1,0:T(8,128)(2,1)S(1)}, bf16[1024,128]{1,0:T(8,128)(2,1)S(1)}, u32[]{:S(2)}, u32[]{:S(2)}) %collective-permute-start.21) | collective-permute-done | bytes 262176 | tf_op jit(solution)/shard_map/ppermute | solution.py:43
  107.3 12.3 %collective-permute-start.30 = (bf16[256,128]{1,0:T(8,128)(2,1)S(1)}, bf16[256,128]{1,0:T(8,128)(2,1)S(1)}, u32[]{:S(2)}, u32[]{:S(2)}) collective-permute-start(bf16[256,128]{1,0:T(8,128)(2,1)S(1)} %get-tuple-element.63.refs_0_), channel_id=1, source_target_pairs={{0,16},{4,20},{8,24},{12,28},{16,0},{20,4},{24,8},{28,12},{1,17},{... | collective-permute-start | bytes 196616 | tf_op jit(solution)/shard_map/ppermute | solution.py:43
  120.9 2.2 %collective-permute-start.38 = (bf16[512,128]{1,0:T(8,128)(2,1)S(1)}, bf16[512,128]{1,0:T(8,128)(2,1)S(1)}, u32[]{:S(2)}, u32[]{:S(2)}) collective-permute-start(bf16[512,128]{1,0:T(8,128)(2,1)S(1)} %get-tuple-element.64.refs_0_), channel_id=1, source_target_pairs={{0,16},{4,20},{8,24},{12,28},{16,0},{20,4},{24,8},{28,12},{1,17},{... | collective-permute-start | bytes 393224 | tf_op jit(solution)/shard_map/ppermute | solution.py:43
  124.5 5.8 %collective-permute-start.32 = (bf16[256,128]{1,0:T(8,128)(2,1)S(1)}, bf16[256,128]{1,0:T(8,128)(2,1)S(1)}, u32[]{:S(2)}, u32[]{:S(2)}) collective-permute-start(bf16[256,128]{1,0:T(8,128)(2,1)S(1)} %get-tuple-element.63.refs_0_), channel_id=1, source_target_pairs={{0,4},{4,0},{8,12},{12,8},{16,20},{20,16},{24,28},{28,24},{1,5},{5... | collective-permute-start | bytes 196616 | tf_op jit(solution)/shard_map/ppermute | solution.py:43
  132.6 5.3 %collective-permute-start.42 = (bf16[512,128]{1,0:T(8,128)(2,1)S(1)}, bf16[512,128]{1,0:T(8,128)(2,1)S(1)}, u32[]{:S(2)}, u32[]{:S(2)}) collective-permute-start(bf16[512,128]{1,0:T(8,128)(2,1)S(1)} %collective-permute-done.38.refs_2_), channel_id=1, source_target_pairs={{0,4},{4,0},{8,12},{12,8},{16,20},{20,16},{24,28},{28,24},{1,5},{5... | collective-permute-start | bytes 393224 | tf_op jit(solution)/shard_map/ppermute | solution.py:43
  138.5 2.1 %shard_map.77.refs_8_ = bf16[1024,768]{1,0:T(8,128)(2,1)S(1)} custom-call(bf16[1024,768]{1,0:T(8,128)(2,1)S(1)} %copy-done.2), custom_call_target="tpu_custom_call" | custom-call | bytes 3145728 | tf_op jit(solution)/shard_map/pallas_call | solution.py:98
  143.1 3.2 %collective-permute-start.44 = (bf16[256,768]{1,0:T(8,128)(2,1)S(1)}, bf16[256,768]{1,0:T(8,128)(2,1)S(1)}, u32[]{:S(2)}, u32[]{:S(2)}) collective-permute-start(bf16[256,768]{1,0:T(8,128)(2,1)S(1)} %get-tuple-element.65), channel_id=1, source_target_pairs={{3,0},{0,1},{1,2},{2,3},{7,4},{4,5},{5,6},{6,7},{11,8},{8,9},{9,10... | collective-permute-start | bytes 1179656 | tf_op jit(solution)/shard_map/ppermute | solution.py:48
  150.0 1.9 %collective-permute-start.24 = (bf16[256,128]{1,0:T(8,128)(2,1)S(1)}, bf16[256,128]{1,0:T(8,128)(2,1)S(1)}, u32[]{:S(2)}, u32[]{:S(2)}) collective-permute-start(bf16[256,128]{1,0:T(8,128)(2,1)S(1)} %get-tuple-element.62.refs_0_), channel_id=1, source_target_pairs={{0,24},{4,28},{8,16},{12,20},{16,8},{20,12},{24,0},{28,4},{1,25},{... | collective-permute-start | bytes 196616 | tf_op jit(solution)/shard_map/ppermute | solution.py:43
  153.1 3.4 %collective-permute-start.25 = (bf16[256,128]{1,0:T(8,128)(2,1)S(1)}, bf16[256,128]{1,0:T(8,128)(2,1)S(1)}, u32[]{:S(2)}, u32[]{:S(2)}) collective-permute-start(bf16[256,128]{1,0:T(8,128)(2,1)S(1)} %get-tuple-element.62.refs_0_), channel_id=1, source_target_pairs={{0,4},{4,0},{8,12},{12,8},{16,20},{20,16},{24,28},{28,24},{1,5},{5... | collective-permute-start | bytes 196616 | tf_op jit(solution)/shard_map/ppermute | solution.py:43
  (98 shorter events, 41.4 us)
Async XLA Ops:
  3.1 27.0 %collective-permute-start.3 = (bf16[768,768]{1,0:T(8,128)(2,1)S(1)}, bf16[768,768]{1,0:T(8,128)(2,1)S(1)}, u32[]{:S(2)}, u32[]{:S(2)}) collective-permute-start(bf16[768,768]{1,0:T(8,128)(2,1)S(1)} %get-tuple-element.39), channel_id=1, source_target_pairs={{0,4},{4,0},{8,12},{12,8},{16,20},{20,16},{24,28},{28,24},{1,5},{5... | collective-permute-start | bytes 3538952 | tf_op jit(solution)/shard_map/ppermute | solution.py:43
  6.4 20.2 %collective-permute-start.7 = (bf16[256,768]{1,0:T(8,128)(2,1)S(1)}, bf16[256,768]{1,0:T(8,128)(2,1)S(1)}, u32[]{:S(2)}, u32[]{:S(2)}) collective-permute-start(bf16[256,768]{1,0:T(8,128)(2,1)S(1)} %copy-done.1), channel_id=1, source_target_pairs={{3,0},{0,1},{1,2},{2,3},{7,4},{4,5},{5,6},{6,7},{11,8},{8,9},{9,10... | collective-permute-start | bytes 1179656 | tf_op jit(solution)/shard_map/ppermute | solution.py:48
  6.4 28.7 %collective-permute-start.2 = (bf16[768,768]{1,0:T(8,128)(2,1)S(1)}, bf16[768,768]{1,0:T(8,128)(2,1)S(1)}, u32[]{:S(2)}, u32[]{:S(2)}) collective-permute-start(bf16[768,768]{1,0:T(8,128)(2,1)S(1)} %get-tuple-element.37), channel_id=1, source_target_pairs={{0,4},{4,0},{8,12},{12,8},{16,20},{20,16},{24,28},{28,24},{1,5},{5... | collective-permute-start | bytes 3538952 | tf_op jit(solution)/shard_map/ppermute | solution.py:43
  6.6 21.0 %collective-permute-start.5 = (bf16[256,768]{1,0:T(8,128)(2,1)S(1)}, bf16[256,768]{1,0:T(8,128)(2,1)S(1)}, u32[]{:S(2)}, u32[]{:S(2)}) collective-permute-start(bf16[256,768]{1,0:T(8,128)(2,1)S(1)} %copy-done.1), channel_id=1, source_target_pairs={{1,0},{2,1},{3,2},{0,3},{5,4},{6,5},{7,6},{4,7},{9,8},{10,9},{11,1... | collective-permute-start | bytes 1179656 | tf_op jit(solution)/shard_map/ppermute | solution.py:48
  9.5 18.1 %collective-permute-start = (bf16[256,768]{1,0:T(8,128)(2,1)S(1)}, bf16[256,768]{1,0:T(8,128)(2,1)S(1)}, u32[]{:S(2)}, u32[]{:S(2)}) collective-permute-start(bf16[256,768]{1,0:T(8,128)(2,1)S(1)} %copy-done.1), channel_id=1, source_target_pairs={{2,0},{3,1},{0,2},{1,3},{6,4},{7,5},{4,6},{5,7},{10,8},{11,9},{8,1... | collective-permute-start | bytes 1179656 | tf_op jit(solution)/shard_map/ppermute | solution.py:48
  31.1 15.8 %collective-permute-start.16 = (bf16[256,768]{1,0:T(8,128)(2,1)S(1)}, bf16[256,768]{1,0:T(8,128)(2,1)S(1)}, u32[]{:S(2)}, u32[]{:S(2)}) collective-permute-start(bf16[256,768]{1,0:T(8,128)(2,1)S(1)} %get-tuple-element.55), channel_id=1, source_target_pairs={{0,8},{4,12},{8,0},{12,4},{16,24},{20,28},{24,16},{28,20},{1,9},{5... | collective-permute-start | bytes 1179656 | tf_op jit(solution)/shard_map/ppermute | solution.py:43
  32.2 23.2 %collective-permute-start.14 = (bf16[256,768]{1,0:T(8,128)(2,1)S(1)}, bf16[256,768]{1,0:T(8,128)(2,1)S(1)}, u32[]{:S(2)}, u32[]{:S(2)}) collective-permute-start(bf16[256,768]{1,0:T(8,128)(2,1)S(1)} %get-tuple-element.52), channel_id=1, source_target_pairs={{0,8},{4,12},{8,0},{12,4},{16,24},{20,28},{24,16},{28,20},{1,9},{5... | collective-permute-start | bytes 1179656 | tf_op jit(solution)/shard_map/ppermute | solution.py:43
  34.8 29.0 %collective-permute-start.12 = (bf16[256,768]{1,0:T(8,128)(2,1)S(1)}, bf16[256,768]{1,0:T(8,128)(2,1)S(1)}, u32[]{:S(2)}, u32[]{:S(2)}) collective-permute-start(bf16[256,768]{1,0:T(8,128)(2,1)S(1)} %get-tuple-element.49), channel_id=1, source_target_pairs={{0,8},{4,12},{8,0},{12,4},{16,24},{20,28},{24,16},{28,20},{1,9},{5... | collective-permute-start | bytes 1179656 | tf_op jit(solution)/shard_map/ppermute | solution.py:43
  36.8 32.0 %collective-permute-start.18 = (bf16[256,384]{1,0:T(8,128)(2,1)S(1)}, bf16[256,384]{1,0:T(8,128)(2,1)S(1)}, u32[]{:S(2)}, u32[]{:S(2)}) collective-permute-start(bf16[256,384]{1,0:T(8,128)(2,1)S(1)} %get-tuple-element.59), channel_id=1, source_target_pairs={{0,16},{4,20},{8,24},{12,28},{16,0},{20,4},{24,8},{28,12},{1,17},{... | collective-permute-start | bytes 589832 | tf_op jit(solution)/shard_map/ppermute | solution.py:43
  39.0 27.2 %collective-permute-start.10 = (f32[8,1408]{1,0:T(8,128)S(1)}, f32[8,1408]{1,0:T(8,128)S(1)}, u32[]{:S(2)}, u32[]{:S(2)}) collective-permute-start(f32[8,1408]{1,0:T(8,128)S(1)} %get-tuple-element.45), channel_id=1, source_target_pairs={{0,16},{4,20},{8,24},{12,28},{16,0},{20,4},{24,8},{28,12},{1,17},{... | collective-permute-start | bytes 135176 | tf_op jit(solution)/shard_map/ppermute | solution.py:43
  46.9 19.4 %collective-permute-start.11 = (f32[8,1408]{1,0:T(8,128)S(1)}, f32[8,1408]{1,0:T(8,128)S(1)}, u32[]{:S(2)}, u32[]{:S(2)}) collective-permute-start(f32[8,1408]{1,0:T(8,128)S(1)} %get-tuple-element.46), channel_id=1, source_target_pairs={{0,24},{4,28},{8,16},{12,20},{16,8},{20,12},{24,0},{28,4},{1,25},{... | collective-permute-start | bytes 135176 | tf_op jit(solution)/shard_map/ppermute | solution.py:43
  55.4 13.0 %collective-permute-start.9 = (f32[8,1408]{1,0:T(8,128)S(1)}, f32[8,1408]{1,0:T(8,128)S(1)}, u32[]{:S(2)}, u32[]{:S(2)}) collective-permute-start(f32[8,1408]{1,0:T(8,128)S(1)} %get-tuple-element.44), channel_id=1, source_target_pairs={{0,8},{4,12},{8,0},{12,4},{16,24},{20,28},{24,16},{28,20},{1,9},{5... | collective-permute-start | bytes 135176 | tf_op jit(solution)/shard_map/ppermute | solution.py:43
  66.2 11.7 %collective-permute-start.20 = (bf16[256,384]{1,0:T(8,128)(2,1)S(1)}, bf16[256,384]{1,0:T(8,128)(2,1)S(1)}, u32[]{:S(2)}, u32[]{:S(2)}) collective-permute-start(bf16[256,384]{1,0:T(8,128)(2,1)S(1)} %get-tuple-element.61), channel_id=1, source_target_pairs={{0,8},{4,12},{8,0},{12,4},{16,24},{20,28},{24,16},{28,20},{1,9},{5... | collective-permute-start | bytes 589832 | tf_op jit(solution)/shard_map/ppermute | solution.py:43
  66.3 23.1 %collective-permute-start.17 = (bf16[256,384]{1,0:T(8,128)(2,1)S(1)}, bf16[256,384]{1,0:T(8,128)(2,1)S(1)}, u32[]{:S(2)}, u32[]{:S(2)}) collective-permute-start(bf16[256,384]{1,0:T(8,128)(2,1)S(1)} %get-tuple-element.57), channel_id=1, source_target_pairs={{0,16},{4,20},{8,24},{12,28},{16,0},{20,4},{24,8},{28,12},{1,17},{... | collective-permute-start | bytes 589832 | tf_op jit(solution)/shard_map/ppermute | solution.py:43
  68.4 25.3 %collective-permute-start.15 = (bf16[256,384]{1,0:T(8,128)(2,1)S(1)}, bf16[256,384]{1,0:T(8,128)(2,1)S(1)}, u32[]{:S(2)}, u32[]{:S(2)}) collective-permute-start(bf16[256,384]{1,0:T(8,128)(2,1)S(1)} %get-tuple-element.54), channel_id=1, source_target_pairs={{0,16},{4,20},{8,24},{12,28},{16,0},{20,4},{24,8},{28,12},{1,17},{... | collective-permute-start | bytes 589832 | tf_op jit(solution)/shard_map/ppermute | solution.py:43
  68.8 29.1 %collective-permute-start.13 = (bf16[256,384]{1,0:T(8,128)(2,1)S(1)}, bf16[256,384]{1,0:T(8,128)(2,1)S(1)}, u32[]{:S(2)}, u32[]{:S(2)}) collective-permute-start(bf16[256,384]{1,0:T(8,128)(2,1)S(1)} %get-tuple-element.51), channel_id=1, source_target_pairs={{0,16},{4,20},{8,24},{12,28},{16,0},{20,4},{24,8},{28,12},{1,17},{... | collective-permute-start | bytes 589832 | tf_op jit(solution)/shard_map/ppermute | solution.py:43
  107.2 15.9 %collective-permute-start.29 = (bf16[256,128]{1,0:T(8,128)(2,1)S(1)}, bf16[256,128]{1,0:T(8,128)(2,1)S(1)}, u32[]{:S(2)}, u32[]{:S(2)}) collective-permute-start(bf16[256,128]{1,0:T(8,128)(2,1)S(1)} %get-tuple-element.63.refs_0_), channel_id=1, source_target_pairs={{0,8},{4,12},{8,0},{12,4},{16,24},{20,28},{24,16},{28,20},{1,9},{5... | collective-permute-start | bytes 196616 | tf_op jit(solution)/shard_map/ppermute | solution.py:43
  107.3 17.1 %collective-permute-start.30 = (bf16[256,128]{1,0:T(8,128)(2,1)S(1)}, bf16[256,128]{1,0:T(8,128)(2,1)S(1)}, u32[]{:S(2)}, u32[]{:S(2)}) collective-permute-start(bf16[256,128]{1,0:T(8,128)(2,1)S(1)} %get-tuple-element.63.refs_0_), channel_id=1, source_target_pairs={{0,16},{4,20},{8,24},{12,28},{16,0},{20,4},{24,8},{28,12},{1,17},{... | collective-permute-start | bytes 196616 | tf_op jit(solution)/shard_map/ppermute | solution.py:43
  120.9 10.8 %collective-permute-start.37 = (bf16[512,128]{1,0:T(8,128)(2,1)S(1)}, bf16[512,128]{1,0:T(8,128)(2,1)S(1)}, u32[]{:S(2)}, u32[]{:S(2)}) collective-permute-start(bf16[512,128]{1,0:T(8,128)(2,1)S(1)} %get-tuple-element.64.refs_0_), channel_id=1, source_target_pairs={{0,8},{4,12},{8,0},{12,4},{16,24},{20,28},{24,16},{28,20},{1,9},{5... | collective-permute-start | bytes 393224 | tf_op jit(solution)/shard_map/ppermute | solution.py:43
  120.9 11.7 %collective-permute-start.38 = (bf16[512,128]{1,0:T(8,128)(2,1)S(1)}, bf16[512,128]{1,0:T(8,128)(2,1)S(1)}, u32[]{:S(2)}, u32[]{:S(2)}) collective-permute-start(bf16[512,128]{1,0:T(8,128)(2,1)S(1)} %get-tuple-element.64.refs_0_), channel_id=1, source_target_pairs={{0,16},{4,20},{8,24},{12,28},{16,0},{20,4},{24,8},{28,12},{1,17},{... | collective-permute-start | bytes 393224 | tf_op jit(solution)/shard_map/ppermute | solution.py:43
  123.2 14.8 %collective-permute-start.39 = (bf16[512,128]{1,0:T(8,128)(2,1)S(1)}, bf16[512,128]{1,0:T(8,128)(2,1)S(1)}, u32[]{:S(2)}, u32[]{:S(2)}) collective-permute-start(bf16[512,128]{1,0:T(8,128)(2,1)S(1)} %get-tuple-element.64.refs_0_), channel_id=1, source_target_pairs={{0,24},{4,28},{8,16},{12,20},{16,8},{20,12},{24,0},{28,4},{1,25},{... | collective-permute-start | bytes 393224 | tf_op jit(solution)/shard_map/ppermute | solution.py:43
  141.2 19.4 %collective-permute-start.36 = (bf16[256,768]{1,0:T(8,128)(2,1)S(1)}, bf16[256,768]{1,0:T(8,128)(2,1)S(1)}, u32[]{:S(2)}, u32[]{:S(2)}) collective-permute-start(bf16[256,768]{1,0:T(8,128)(2,1)S(1)} %shard_map.79), channel_id=1, source_target_pairs={{2,0},{3,1},{0,2},{1,3},{6,4},{7,5},{4,6},{5,7},{10,8},{11,9},{8,1... | collective-permute-start | bytes 1179656 | tf_op jit(solution)/shard_map/ppermute | solution.py:48
  143.1 19.2 %collective-permute-start.44 = (bf16[256,768]{1,0:T(8,128)(2,1)S(1)}, bf16[256,768]{1,0:T(8,128)(2,1)S(1)}, u32[]{:S(2)}, u32[]{:S(2)}) collective-permute-start(bf16[256,768]{1,0:T(8,128)(2,1)S(1)} %get-tuple-element.65), channel_id=1, source_target_pairs={{3,0},{0,1},{1,2},{2,3},{7,4},{4,5},{5,6},{6,7},{11,8},{8,9},{9,10... | collective-permute-start | bytes 1179656 | tf_op jit(solution)/shard_map/ppermute | solution.py:48
  146.3 16.5 %collective-permute-start.45 = (bf16[256,768]{1,0:T(8,128)(2,1)S(1)}, bf16[256,768]{1,0:T(8,128)(2,1)S(1)}, u32[]{:S(2)}, u32[]{:S(2)}) collective-permute-start(bf16[256,768]{1,0:T(8,128)(2,1)S(1)} %get-tuple-element.66), channel_id=1, source_target_pairs={{1,0},{2,1},{3,2},{0,3},{5,4},{6,5},{7,6},{4,7},{9,8},{10,9},{11,1... | collective-permute-start | bytes 1179656 | tf_op jit(solution)/shard_map/ppermute | solution.py:48
  (28 other events, 187.3 us)
